TPU v7x, 32 devices: a whole 2x2x4 slice. The times are simulated.
32 devices in a mesh: dp: 8 (over y, x, core), tensor: 4 (over z).
Axes of the slice: x: 2, y: 2, z: 4, core: 2. Of those that a mesh axis runs over, the one named last changes fastest.
Arguments:
- tokens: bfloat16 [8192, 1024], P(('dp', 'tensor')), may hold values from -6 to 6
- cotangent: bfloat16 [8192, 1024], P(('dp', 'tensor')), may hold values from -6 to 6
- positions: int32 [8, 1024], P('dp', 'tensor'), may hold values from 0 to 4095
- segment_ids: int32 [8, 1024], P('dp'), may hold values from 0 to 3, as said below
- spatial_flag: int32 [8, 4], P('dp'), may hold values from 0 to 1
- attn_weight: float32 [4, 1024, 1024], P(None, 'dp', 'tensor'), may hold values from -6 to 6
- attn_moments: float32 [2, 4, 1024, 1024], P(None, None, 'dp', 'tensor'), may hold values from -5 to 5, as said below
- attn_ema: float32 [4, 1024, 1024], P(None, 'dp', 'tensor'), may hold values from -6 to 6
- ffn_weight: float32 [2, 1024, 4096], P(None, 'dp', 'tensor'), may hold values from -6 to 6
- ffn_moments: float32 [2, 2, 1024, 4096], P(None, None, 'dp', 'tensor'), may hold values from -5 to 5, as said below
- ffn_ema: float32 [2, 1024, 4096], P(None, 'dp', 'tensor'), may hold values from -6 to 6
- norm_weight: float32 [4, 1024], replicated, may hold values from -0.3 to 1.5, as said below
- norm_moments: float32 [2, 4, 1024], replicated, may hold values from -5 to 5, as said below
- norm_ema: float32 [4, 1024], replicated, may hold values from -0.3 to 1.5, as said below
Outputs:
- out_tokens: bfloat16 [8192, 1024], P(('dp', 'tensor'))
- grad_tokens: bfloat16 [8192, 1024], P(('dp', 'tensor'))
- attn_grad: float32 [4, 1024, 1024], P(None, 'dp', 'tensor')
- ffn_grad: float32 [2, 1024, 4096], P(None, 'dp', 'tensor')
- norm_grad: float32 [4, 1024], replicated
- attn_new: float32 [4, 1024, 1024], P(None, 'dp', 'tensor')
- attn_mom_new: float32 [2, 4, 1024, 1024], P(None, None, 'dp', 'tensor')
- attn_ema_new: float32 [4, 1024, 1024], P(None, 'dp', 'tensor')
- ffn_new: float32 [2, 1024, 4096], P(None, 'dp', 'tensor')
- ffn_mom_new: float32 [2, 2, 1024, 4096], P(None, None, 'dp', 'tensor')
- ffn_ema_new: float32 [2, 1024, 4096], P(None, 'dp', 'tensor')
- norm_new: float32 [4, 1024], replicated
- norm_mom_new: float32 [2, 4, 1024], replicated
- norm_ema_new: float32 [4, 1024], replicated
Inputs may be any that keep to these rules, and one draw needn't show every extreme that they name: `segment_ids`: items are contiguous runs of cells numbered in order from 0 within each group; every item has at least one cell. `attn_moments`: entry 0 of the first dimension is the first moment, entry 1 the second moment, which is positive. `ffn_moments`: entry 0 of the first dimension is the first moment, entry 1 the second moment, which is positive. `norm_moments`: entry 0 of the first dimension is the first moment, entry 1 the second moment, which is positive. `norm_weight`: rows 0 and 2 are gains between 0.5 and 1.5, rows 1 and 3 biases. `norm_ema`: rows 0 and 2 are gains between 0.5 and 1.5, rows 1 and 3 biases.
All inputs are finite; a program needn't handle non-finite values.
Results may differ from a plain program's by a relative error of at most 0.012.
Values may be sent and summed in bfloat16 or wider, within the bound.
A program may use at most 128 MiB of HBM per device.

v0:
```python
import jax
import jax.numpy as jnp
from jax import lax
from jax.sharding import PartitionSpec as P

HD = 64
FF = 4096
STEP = 5


out_gain = 16.0
beta_one = 0.6
beta_two = 0.95
adam_eps = 1e-08
decay_rate = 0.1
learn_value = 0.25
ema_value = 0.7
norm_eps = 1e-05
masked_score = -1e30


def sinusoid(cell_pos, model_width):
    feature = jnp.arange(model_width, dtype=jnp.int32)
    freqs = jnp.power(10000.0, -(2 * (feature // 2)).astype(jnp.float32) / model_width)
    angles = cell_pos.astype(jnp.float32)[:, None] * freqs[None, :]
    return jnp.where(feature % 2 == 0, jnp.sin(angles), jnp.cos(angles))


def layer_norm(inputs, gain_vec, bias_vec):
    row_mean = jnp.mean(inputs, axis=-1, keepdims=True)
    centred = inputs - row_mean
    row_var = jnp.mean(centred * centred, axis=-1, keepdims=True)
    return centred * lax.rsqrt(row_var + norm_eps) * gain_vec + bias_vec


def exact_gelu(values):
    return jax.nn.gelu(values, approximate=False)


def adam_update(weight, moments, ema_weight, gradient):
    step_num = float(STEP)
    first_mom = beta_one * moments[0] + (1.0 - beta_one) * gradient
    second_mom = beta_two * moments[1] + (1.0 - beta_two) * gradient * gradient
    fix_one = 1.0 - beta_one**step_num
    fix_two = 1.0 - beta_two**step_num
    update = first_mom / fix_one / (jnp.sqrt(second_mom / fix_two) + adam_eps) + decay_rate * weight
    new_weight = weight - learn_value * update
    new_ema = ema_value * ema_weight + (1.0 - ema_value) * new_weight
    return (new_weight, jnp.stack([first_mom, second_mom]), new_ema)


def dot_last(left, right):
    return lax.dot_general(
        left, right, (((1,), (1,)), ((), ())), preferred_element_type=jnp.float32
    )


def dot_first(left, right):
    return lax.dot_general(
        left, right, (((0,), (0,)), ((), ())), preferred_element_type=jnp.float32
    )


def local(
    tokens,
    cotangent,
    positions,
    segment_ids,
    spatial_flag,
    attn_weight,
    attn_moments,
    attn_ema,
    ffn_weight,
    ffn_moments,
    ffn_ema,
    norm_weight,
    norm_moments,
    norm_ema,
):
    tok_rows = tokens.shape[0]
    model_width = tokens.shape[1]
    seg_all = segment_ids[0]
    group_len = seg_all.shape[0]
    q_block = min(512, group_len)
    block_count = group_len // q_block
    scale_d = model_width ** (-0.5)
    scale_f = FF ** (-0.5)
    score_scale = HD ** (-0.5)
    out_scale = out_gain * scale_d
    grad_scale = float(group_len * lax.axis_size("dp")) ** (-0.5)
    row_first = lax.axis_index("tensor") * tok_rows
    seg_own = lax.dynamic_slice_in_dim(seg_all, row_first, tok_rows, 0)
    item_ids = jnp.arange(spatial_flag.shape[1], dtype=jnp.int32)
    cell_flag = jnp.sum(
        jnp.where(seg_own[:, None] == item_ids[None, :], spatial_flag[0][None, :], 0), axis=1
    )
    x_embed = tokens.astype(jnp.float32) + cell_flag.astype(jnp.float32)[:, None] * sinusoid(
        positions[0], model_width
    )
    attn_half, ffn_half = (
        lax.all_gather(attn_weight.astype(jnp.bfloat16), "dp", axis=1, tiled=True),
        lax.all_gather(ffn_weight.astype(jnp.bfloat16), "dp", axis=1, tiled=True),
    )
    head_width = attn_half.shape[2]
    head_count = head_width // HD
    h_one_f, norm_one_pull = jax.vjp(layer_norm, x_embed, norm_weight[0], norm_weight[1])
    h_one = lax.all_gather(h_one_f.astype(jnp.bfloat16), "tensor", axis=0, tiled=True)
    projected = (
        jnp.einsum("gd,cdj->cgj", h_one, attn_half[:3], preferred_element_type=jnp.float32)
        * scale_d
    ).astype(jnp.bfloat16)
    queries = projected[0].reshape(group_len, head_count, HD)
    key_rows = projected[1].reshape(group_len, head_count, HD)
    val_rows = projected[2].reshape(group_len, head_count, HD)

    def score_block(block_index):
        row_start = block_index * q_block
        query_blk = lax.dynamic_slice_in_dim(queries, row_start, q_block, 0)
        seg_blk = lax.dynamic_slice_in_dim(seg_all, row_start, q_block, 0)
        scores = (
            jnp.einsum("qhd,khd->hqk", query_blk, key_rows, preferred_element_type=jnp.float32)
            * score_scale
        )
        allowed = (seg_blk[:, None] == seg_all[None, :])[None]
        return (query_blk, jnp.where(allowed, scores, masked_score), allowed)

    def attend(block_index):
        query_blk, scores, allowed = score_block(block_index)
        row_top = jnp.max(scores, axis=2, keepdims=True)
        exp_rows = jnp.exp(scores - row_top)
        row_total = jnp.sum(exp_rows, axis=2, keepdims=True)
        prob_rows = (exp_rows / row_total).astype(jnp.bfloat16)
        result = jnp.einsum("hqk,khd->qhd", prob_rows, val_rows, preferred_element_type=jnp.float32)
        return (result, (row_top + jnp.log(row_total))[:, :, 0])

    attended, log_totals = lax.map(attend, jnp.arange(block_count))
    attended = attended.reshape(group_len, head_width).astype(jnp.bfloat16)
    branch = lax.psum_scatter(
        dot_last(attended, attn_half[3]) * out_scale, "tensor", scatter_dimension=0, tiled=True
    )
    x_mid = x_embed + branch
    h_two_f, norm_two_pull = jax.vjp(layer_norm, x_mid, norm_weight[2], norm_weight[3])
    h_two = lax.all_gather(h_two_f.astype(jnp.bfloat16), "tensor", axis=0, tiled=True)
    hidden = jnp.dot(h_two, ffn_half[0], preferred_element_type=jnp.float32) * scale_d
    activated_f, gelu_pull = jax.vjp(exact_gelu, hidden)
    activated = activated_f.astype(jnp.bfloat16)
    ffn_out = lax.psum_scatter(
        dot_last(activated, ffn_half[1]) * scale_f, "tensor", scatter_dimension=0, tiled=True
    )
    out_tokens = (x_mid + ffn_out).astype(jnp.bfloat16)
    dy_own = cotangent.astype(jnp.float32)
    dy_all = lax.all_gather(cotangent, "tensor", axis=0, tiled=True)
    d_act = jnp.dot(dy_all, ffn_half[1], preferred_element_type=jnp.float32) * scale_f
    d_hidden = gelu_pull(d_act)[0].astype(jnp.bfloat16)
    grad_down = dot_first(dy_all, activated) * scale_f
    grad_up = dot_first(h_two, d_hidden) * scale_d
    d_h_two = lax.psum_scatter(
        dot_last(d_hidden, ffn_half[0]) * scale_d, "tensor", scatter_dimension=0, tiled=True
    )
    d_mid_part, d_gain_two, d_bias_two = norm_two_pull(d_h_two)
    d_mid = dy_own + d_mid_part
    d_mid_all = lax.all_gather(d_mid.astype(jnp.bfloat16), "tensor", axis=0, tiled=True)
    d_att = (
        jnp.dot(d_mid_all, attn_half[3], preferred_element_type=jnp.float32) * out_scale
    ).astype(jnp.bfloat16)
    grad_mix = dot_first(d_mid_all, attended) * out_scale
    d_att3 = d_att.reshape(group_len, head_count, HD)

    def attend_back(state_pair, block_index):
        dk_sum, dv_sum = state_pair
        query_blk, scores, allowed = score_block(block_index)
        row_start = block_index * q_block
        dout_blk = lax.dynamic_slice_in_dim(d_att3, row_start, q_block, 0)
        prob_rows = jnp.where(allowed, jnp.exp(scores - log_totals[block_index][:, :, None]), 0.0)
        dv_sum = dv_sum + jnp.einsum(
            "hqk,qhd->khd",
            prob_rows.astype(jnp.bfloat16),
            dout_blk,
            preferred_element_type=jnp.float32,
        )
        d_prob = jnp.einsum("qhd,khd->hqk", dout_blk, val_rows, preferred_element_type=jnp.float32)
        d_score = (
            prob_rows * (d_prob - jnp.sum(d_prob * prob_rows, axis=2, keepdims=True))
        ).astype(jnp.bfloat16)
        dq_blk = (
            jnp.einsum("hqk,khd->qhd", d_score, key_rows, preferred_element_type=jnp.float32)
            * score_scale
        )
        dk_sum = (
            dk_sum
            + jnp.einsum("hqk,qhd->khd", d_score, query_blk, preferred_element_type=jnp.float32)
            * score_scale
        )
        return ((dk_sum, dv_sum), dq_blk)

    zero_keys = jnp.zeros((group_len, head_count, HD), jnp.float32)
    (dk_sum, dv_sum), dq_blocks = lax.scan(
        attend_back, (zero_keys, zero_keys), jnp.arange(block_count)
    )
    d_proj = jnp.stack(
        [
            dq_blocks.reshape(group_len, head_width),
            dk_sum.reshape(group_len, head_width),
            dv_sum.reshape(group_len, head_width),
        ]
    ).astype(jnp.bfloat16)
    grad_proj = (
        jnp.einsum("gd,cgj->cdj", h_one, d_proj, preferred_element_type=jnp.float32) * scale_d
    )
    d_h_one = lax.psum_scatter(
        jnp.einsum("cgj,cdj->gd", d_proj, attn_half[:3], preferred_element_type=jnp.float32)
        * scale_d,
        "tensor",
        scatter_dimension=0,
        tiled=True,
    )
    d_embed_part, d_gain_one, d_bias_one = norm_one_pull(d_h_one)
    grad_tokens = (d_mid + d_embed_part).astype(jnp.bfloat16)
    attn_part = jnp.concatenate([grad_proj, grad_mix[None]], axis=0)
    ffn_part = jnp.stack([grad_up, grad_down])
    attn_grad, ffn_grad = (
        lax.psum_scatter(attn_part, "dp", scatter_dimension=1, tiled=True),
        lax.psum_scatter(ffn_part, "dp", scatter_dimension=1, tiled=True),
    )
    norm_grad = lax.psum(
        jnp.stack([d_gain_one, d_bias_one, d_gain_two, d_bias_two]), ("dp", "tensor")
    )
    attn_new, attn_mom_new, attn_ema_new = adam_update(
        attn_weight, attn_moments, attn_ema, attn_grad * grad_scale
    )
    ffn_new, ffn_mom_new, ffn_ema_new = adam_update(
        ffn_weight, ffn_moments, ffn_ema, ffn_grad * grad_scale
    )
    norm_new, norm_mom_new, norm_ema_new = adam_update(
        norm_weight, norm_moments, norm_ema, norm_grad * grad_scale
    )
    return (
        out_tokens,
        grad_tokens,
        attn_grad,
        ffn_grad,
        norm_grad,
        attn_new,
        attn_mom_new,
        attn_ema_new,
        ffn_new,
        ffn_mom_new,
        ffn_ema_new,
        norm_new,
        norm_mom_new,
        norm_ema_new,
    )


def solution(mesh):
    placed = (
        P(("dp", "tensor"), None),
        P(("dp", "tensor"), None),
        P("dp", "tensor"),
        P("dp", None),
        P("dp", None),
        P(None, "dp", "tensor"),
        P(None, None, "dp", "tensor"),
        P(None, "dp", "tensor"),
        P(None, "dp", "tensor"),
        P(None, None, "dp", "tensor"),
        P(None, "dp", "tensor"),
        P(),
        P(),
        P(),
    )
    return jax.shard_map(
        local,
        mesh=mesh,
        in_specs=placed,
        out_specs=(
            P(("dp", "tensor"), None),
            P(("dp", "tensor"), None),
            P(None, "dp", "tensor"),
            P(None, "dp", "tensor"),
            P(),
            P(None, "dp", "tensor"),
            P(None, None, "dp", "tensor"),
            P(None, "dp", "tensor"),
            P(None, "dp", "tensor"),
            P(None, None, "dp", "tensor"),
            P(None, "dp", "tensor"),
            P(),
            P(),
            P(),
        ),
        check_vma=False,
    )
```

profile of v0, /device:TPU:5, one launch (start us, length us, event | category | flops | bytes accessed | tf_op | source)
XLA Modules:
  0.0 838.0 jit_solution(9046201732425459849)
XLA Ops:
  9.4 5.1 fusion.58
  15.4 5.3 multiply_reduce_fusion.6
  22.2 1.6 copy.115
  27.1 44.9 %all-gather.7.cloned.1.call-done = bf16[1024,1024]{1,0:T(8,128)(2,1)} async-done(((bf16[256,1024]{1,0:T(8,128)(2,1)}), bf16[1024,1024]{1,0:T(8,128)(2,1)}) %all-gather.7.cloned.1.call-update) | async-done | bytes 2097168 | tf_op jit(solution)/shard_map/all_gather | solution.py:107
  72.0 29.5 %all-gather.9.cloned.1.call-done = bf16[4,1024,256]{1,2,0:T(8,128)(2,1)} async-done(((bf16[4,128,256]{1,2,0:T(8,128)(2,1)}), bf16[4,1024,256]{1,2,0:T(8,128)(2,1)}) %all-gather.9.cloned.1.call-update) | async-done | bytes 2097168 | tf_op jit(solution)/shard_map/all_gather | solution.py:101
  101.5 3.9 fusion.46
  105.5 17.6 %while.27 = (s32[]{:T(128)}, bf16[2,512,4,64]{1,3,2,0:T(8,128)(2,1)S(1)}, f32[2,4,512]{2,1,0:T(4,128)S(1)}, s32[2]{0:T(128)S(1)}, s32[1024]{0:T(1024)S(1)}, /*in...) while((s32[]{:T(128)}, ...), condition=%wide.region_6.7_spmd, body=%wide.region_3.6_spmd.sunk | while | flops 562558976 | bytes 29173968 | solution.py:136
  107.2 1.7 fusion.129
  108.9 2.3 fusion.130
  111.3 3.0 fusion.131
  116.0 1.7 fusion.129
  117.7 2.3 fusion.130
  120.1 3.0 fusion.131
  124.6 3.8 convolution_multiply_fusion.4
  130.6 74.7 %reduce-scatter.7.cloned.1.call-done = f32[256,1024]{0,1:T(8,128)} async-done(((f32[1024,1024]{0,1:T(8,128)}), f32[256,1024]{0,1:T(8,128)}) %reduce-scatter.7.cloned.1.call-update) | async-done | bytes 1048592 | tf_op jit(solution)/shard_map/reduce_scatter | solution.py:138
  205.3 1.6 copy.119
  206.8 5.2 fusion.84
  214.0 31.2 %all-gather.13.cloned.1.call-done = bf16[2,1024,1024]{2,1,0:T(8,128)(2,1)} async-done(((bf16[2,128,1024]{2,1,0:T(8,128)(2,1)}), bf16[2,1024,1024]{2,1,0:T(8,128)(2,1)}) %all-gather.13.cloned.1.call-update) | async-done | bytes 4194320 | tf_op jit(solution)/shard_map/all_gather | solution.py:102
  245.2 47.8 %all-gather.11.cloned.1.call-done = bf16[1024,1024]{1,0:T(8,128)(2,1)} async-done(((bf16[256,1024]{1,0:T(8,128)(2,1)}), bf16[1024,1024]{1,0:T(8,128)(2,1)}) %all-gather.11.cloned.1.call-update) | async-done | bytes 2097168 | tf_op jit(solution)/shard_map/all_gather | solution.py:143
  293.0 15.5 %multiply_convert_fusion.1 = (bf16[1024,1024]{0,1:T(8,128)(2,1)}, f32[1024,1024]{0,1:T(8,128)}, f32[1024,1024]{0,1:T(8,128)}) fusion(bf16[1024,1024]{1,0:T(8,128)(2,1)} %all-gather.11.cloned.1.call-done, bf16[2,1024,1024]{2,1,0:T(8,128)(2,1)} %all-gather.13.cloned.1.call-done), kind=kOutput, calls=%fused_computation.47 | convolution fusion | flops 2216689664 | bytes 14680064 | tf_op jit(solution)/shard_map/dot_general | solution.py:144
  308.5 30.7 %all-gather.15.cloned.1.call-done = bf16[1024,1024]{1,0:T(8,128)(2,1)} async-done(((bf16[256,1024]{1,0:T(8,128)(2,1)}), bf16[1024,1024]{1,0:T(8,128)(2,1)}) %all-gather.15.cloned.1.call-update) | async-done | bytes 2097168 | tf_op jit(solution)/shard_map/all_gather | solution.py:152
  339.2 8.8 %add_convert_fusion = bf16[1024,1024]{0,1:T(8,128)(2,1)S(1)} fusion(f32[1024,1024]{0,1:T(8,128)} %get-tuple-element.272, f32[1024,1024]{0,1:T(8,128)} %get-tuple-element.301, bf16[1024,1024]{1,0:T(8,128)(2,1)} %all-gather.15.cloned.1.call-done, bf16[2,1024,1024]{2,1,0:T(8,128)(2,1)} %all-gather.13.cloned.1.call-done), kind=kOutput, calls=%fused_computation.46 | convolution fusion | flops 2164260864 | bytes 14680064 | tf_op jit(solution)/shard_map/dot_general | solution.py:153
  349.4 4.3 convolution_multiply_fusion.2
  353.7 5.4 copy.126
  359.7 6.6 convolution_multiply_fusion.3
  366.3 68.6 %reduce-scatter.11.cloned.1.call-done = f32[256,1024]{1,0:T(8,128)} async-done(((f32[1024,1024]{1,0:T(8,128)}), f32[256,1024]{1,0:T(8,128)}) %reduce-scatter.11.cloned.1.call-update) | async-done | bytes 1048592 | tf_op jit(solution)/shard_map/reduce_scatter | solution.py:157
  434.9 2.2 multiply_reduce_fusion.1
  437.1 77.4 %reduce-scatter.9.cloned.1.call-done = f32[256,1024]{1,0:T(8,128)} async-done(((f32[1024,1024]{1,0:T(8,128)}), f32[256,1024]{1,0:T(8,128)}) %reduce-scatter.9.cloned.1.call-update) | async-done | bytes 1048592 | tf_op jit(solution)/shard_map/reduce_scatter | solution.py:147
  514.5 2.7 fusion.82
  519.4 4.7 multiply_bitcast_fusion
  524.1 2.3 multiply_bitcast_fusion.1
  526.5 4.1 pad_maximum_fusion
  530.9 35.0 %all-gather.17.cloned.1.call-done = bf16[1024,1024]{1,0:T(8,128)(2,1)} async-done(((bf16[256,1024]{1,0:T(8,128)(2,1)}), bf16[1024,1024]{1,0:T(8,128)(2,1)}) %all-gather.17.cloned.1.call-update) | async-done | bytes 2097168 | tf_op jit(solution)/shard_map/all_gather | solution.py:162
  565.9 3.2 fusion.52
  569.9 27.4 %while.28 = (s32[]{:T(128)}, f32[1024,4,64]{0,2,1:T(8,128)S(1)}, f32[1024,4,64]{0,2,1:T(8,128)S(1)}, bf16[2,512,4,64]{1,3,2,0:T(8,128)(2,1)}, s32[2]{0:T(128)S(1...) while((s32[]{:T(128)}, f32[1024,4,64]{0,2,1:T(8,128)S(1)}, ...), condition=%wide.region_16.17_spmd.clone, body=%wide.region_14.16_spmd.clone.sunk | while | flops 1365112832 | bytes 79743384 | solution.py:197
  573.6 3.9 exponential_select_fusion.2
  578.5 1.5 multiply_reduce_fusion.8
  587.3 3.9 exponential_select_fusion.2
  597.3 2.4 copy.167
  599.7 2.7 reshape.234
  603.0 2.3 fusion.51
  605.3 3.4 multiply_bitcast_fusion.2
  608.8 2.3 pad_maximum_fusion.1
  611.3 5.2 bitcast_multiply_fusion
  618.1 2.0 copy.144
  623.8 3.1 fusion.87
  626.9 1.5 copy.172
  628.5 2.5 copy.173
  631.0 8.5 %reduce-scatter.17.cloned.1.call-done = f32[2,128,1024]{1,2,0:T(8,128)} async-done(((f32[2,1024,1024]{1,2,0:T(8,128)}), f32[2,128,1024]{1,2,0:T(8,128)}) %reduce-scatter.17.cloned.1.call-update) | async-done | bytes 1048592 | tf_op jit(solution)/shard_map/reduce_scatter | solution.py:223
  639.5 4.5 multiply_add_fusion
  644.0 2.5 copy.157
  646.5 2.5 copy.155
  649.0 1.7 pad_maximum_fusion.2
  650.8 1.8 copy.156
  652.6 2.6 copy.151
  655.2 39.0 %reduce-scatter.15.cloned.1.call-done = f32[4,128,256]{1,2,0:T(8,128)} async-done(((f32[4,1024,256]{1,2,0:T(8,128)}), f32[4,128,256]{1,2,0:T(8,128)}) %reduce-scatter.15.cloned.1.call-update) | async-done | bytes 524304 | tf_op jit(solution)/shard_map/reduce_scatter | solution.py:222
  694.3 2.6 multiply_add_fusion.2
  701.3 2.1 copy.150
  703.4 70.0 %reduce-scatter.13.cloned.1.call-done = f32[256,1024]{0,1:T(8,128)} async-done(((f32[1024,1024]{0,1:T(8,128)}), f32[256,1024]{0,1:T(8,128)}) %reduce-scatter.13.cloned.1.call-update) | async-done | bytes 1048592 | tf_op jit(solution)/shard_map/reduce_scatter | solution.py:210
  773.4 2.5 copy.133
  777.4 1.6 multiply_reduce_fusion.2
  779.0 39.9 %psum.7 = f32[4,1024]{1,0:T(4,128)S(1)} all-reduce(f32[4,1024]{1,0:T(4,128)S(1)} %pad_maximum_fusion.8), channel_id=1, replica_groups=mesh['dp'=8,'tensor'=4] {'dp','tensor'}, use_global_device_ids=true, to_apply=%region_26.27 | all-reduce | flops 4096 | bytes 32768 | tf_op jit(solution)/shard_map/psum | solution.py:225
  821.7 2.7 multiply_add_fusion.1
  824.5 2.6 copy.136
  (195 shorter events, 51.8 us)
Async XLA Ops:
  7.2 64.8 %all-gather.7.cloned.1.call-start = ((), (), s32[]{:S(2)}) async-start(), calls=%async_computation.6 | async-start | bytes 2621440 | tf_op jit(solution)/shard_map/all_gather | solution.py:107
  15.4 9.3 %copy-start.25 = (f32[1,1024]{1,0:T(1,128)}, f32[1,1024]{1,0:T(1,128)S(1)}, u32[]{:S(2)}) copy-start(f32[1,1024]{1,0:T(1,128)S(1)} %get-tuple-element.299) | copy-start | bytes 12292
  20.7 4.0 copy-start
  20.7 4.0 copy-start.35
  20.7 4.0 copy-start.28
  21.0 5.8 copy-start.5
  24.7 76.8 %all-gather.9.cloned.1.call-start = ((), (), s32[]{:S(2)}) async-start(), calls=%async_computation.7 | async-start | bytes 2359296 | tf_op jit(solution)/shard_map/all_gather | solution.py:101
  26.0 75.5 %copy-start.11 = (f32[4,128,256]{1,2,0:T(8,128)}, f32[4,128,256]{1,2,0:T(8,128)S(1)}, u32[]{:S(2)}) copy-start(f32[4,128,256]{1,2,0:T(8,128)S(1)} %copy.116) | copy-start | bytes 1572868
  26.8 178.4 %reduce-scatter.7.cloned.1.call-start = ((), (), s32[]{:S(2)}) async-start(), calls=%async_computation.8 | async-start | bytes 5242880 | tf_op jit(solution)/shard_map/reduce_scatter | solution.py:138
  27.1 78.5 %copy-start.21 = (s32[1,1024]{1,0:T(1,128)S(1)}, s32[1,1024]{1,0:T(1,128)}, u32[]{:S(2)}) copy-start(s32[1,1024]{1,0:T(1,128)} %param.21) | copy-start | bytes 12292
  123.1 5.3 copy-start.2
  123.8 0.8 copy-start.9
  128.4 1.2 copy-start.15
  128.4 116.8 %all-gather.13.cloned.1.call-start = ((), (), s32[]{:S(2)}) async-start(), calls=%async_computation.10 | async-start | bytes 4718592 | tf_op jit(solution)/shard_map/all_gather | solution.py:102
  130.5 162.5 %all-gather.11.cloned.1.call-start = ((), (), s32[]{:S(2)}) async-start(), calls=%async_computation.9 | async-start | bytes 2621440 | tf_op jit(solution)/shard_map/all_gather | solution.py:143
  213.4 125.8 %all-gather.15.cloned.1.call-start = ((), (), s32[]{:S(2)}) async-start(), calls=%async_computation.12 | async-start | bytes 2621440 | tf_op jit(solution)/shard_map/all_gather | solution.py:152
  214.0 220.9 %reduce-scatter.11.cloned.1.call-start = ((), (), s32[]{:S(2)}) async-start(), calls=%async_computation.13 | async-start | bytes 5242880 | tf_op jit(solution)/shard_map/reduce_scatter | solution.py:157
  339.2 10.2 %copy-start.37 = (bf16[2,1024,1024]{2,1,0:T(8,128)(2,1)S(1)}, bf16[2,1024,1024]{2,1,0:T(8,128)(2,1)}, u32[]{:S(2)}) copy-start(bf16[2,1024,1024]{2,1,0:T(8,128)(2,1)} %all-gather.13.cloned.1.call-done) | copy-start | bytes 12582916
  348.1 1.4 copy-start.39
  359.2 155.3 %reduce-scatter.9.cloned.1.call-start = ((), (), s32[]{:S(2)}) async-start(), calls=%async_computation.11 | async-start | bytes 5242880 | tf_op jit(solution)/shard_map/reduce_scatter | solution.py:147
  366.3 152.0 %copy-start.13 = (bf16[256,1024]{1,0:T(8,128)(2,1)S(1)}, bf16[256,1024]{1,0:T(8,128)(2,1)}, u32[]{:S(2)}) copy-start(bf16[256,1024]{1,0:T(8,128)(2,1)} %param.19) | copy-start | bytes 1572868
  366.3 199.6 %all-gather.17.cloned.1.call-start = ((), (), s32[]{:S(2)}) async-start(), calls=%async_computation.14 | async-start | bytes 2621440 | tf_op jit(solution)/shard_map/all_gather | solution.py:162
  517.2 1.1 copy-start.7
  517.2 6.9 copy-start.33
  519.3 120.2 %reduce-scatter.17.cloned.1.call-start = ((), (), s32[]{:S(2)}) async-start(), calls=%async_computation.17 | async-start | bytes 9437184 | tf_op jit(solution)/shard_map/reduce_scatter | solution.py:223
  519.4 4.7 copy-start.38
  519.4 4.7 copy-start.40
  530.6 163.7 %reduce-scatter.15.cloned.1.call-start = ((), (), s32[]{:S(2)}) async-start(), calls=%async_computation.16 | async-start | bytes 4718592 | tf_op jit(solution)/shard_map/reduce_scatter | solution.py:222
  573.5 4.0 copy-start.4
  580.0 1.2 copy-start.18
  581.2 1.4 copy-start.3
  582.6 1.0 copy-start.19
  587.3 3.9 copy-start.4
  593.7 1.2 copy-start.18
  594.9 1.4 copy-start.3
  596.3 1.0 copy-start.19
  597.3 5.7 copy-start.10
  602.5 2.8 copy-start.22
  611.1 162.3 %reduce-scatter.13.cloned.1.call-start = ((), (), s32[]{:S(2)}) async-start(), calls=%async_computation.15 | async-start | bytes 5242880 | tf_op jit(solution)/shard_map/reduce_scatter | solution.py:210
  616.6 1.2 copy-start.16
  616.6 3.6 copy-start.20
  650.7 43.5 %copy-start.12 = (f32[4,128,256]{1,2,0:T(8,128)S(1)}, f32[4,128,256]{1,2,0:T(8,128)}, u32[]{:S(2)}) copy-start(f32[4,128,256]{1,2,0:T(8,128)} %copy-done.11) | copy-start | bytes 1572868
  650.8 43.5 %copy-start.17 = (f32[4,128,256]{1,2,0:T(8,128)S(1)}, f32[4,128,256]{1,2,0:T(8,128)}, u32[]{:S(2)}) copy-start(f32[4,128,256]{1,2,0:T(8,128)} %copy.144) | copy-start | bytes 1572868
  697.9 78.1 %copy-start.1 = (f32[256,1024]{1,0:T(8,128)S(1)}, f32[256,1024]{1,0:T(8,128)}, u32[]{:S(2)}) copy-start(f32[256,1024]{1,0:T(8,128)} %copy-done) | copy-start | bytes 3145732
  697.9 78.1 %copy-start.26 = (f32[1,1024]{1,0:T(1,128)S(1)}, f32[1,1024]{1,0:T(1,128)}, u32[]{:S(2)}) copy-start(f32[1,1024]{1,0:T(1,128)} %copy-done.25) | copy-start | bytes 12292
  700.0 77.4 %copy-start.36 = (f32[256]{0:T(256)S(1)}, f32[256]{0:T(256)}, u32[]{:S(2)}) copy-start(f32[256]{0:T(256)} %copy-done.35) | copy-start | bytes 3076
  700.0 77.4 %copy-start.6 = (f32[256,1024]{0,1:T(8,128)S(1)}, f32[256,1024]{0,1:T(8,128)}, u32[]{:S(2)}) copy-start(f32[256,1024]{0,1:T(8,128)} %copy-done.5) | copy-start | bytes 3145732
  700.0 77.4 %copy-start.29 = (f32[256]{0:T(256)S(1)}, f32[256]{0:T(256)}, u32[]{:S(2)}) copy-start(f32[256]{0:T(256)} %copy-done.28) | copy-start | bytes 3076
  701.3 77.7 %copy-start.30 = (f32[1024]{0:T(1024)S(1)}, f32[1024]{0:T(1024)}, u32[]{:S(2)}) copy-start(f32[1024]{0:T(1024)} %get-tuple-element.212) | copy-start | bytes 12292
  701.3 77.7 %copy-start.31 = (f32[1024]{0:T(1024)S(1)}, f32[1024]{0:T(1024)}, u32[]{:S(2)}) copy-start(f32[1024]{0:T(1024)} %get-tuple-element.216) | copy-start | bytes 12292
  818.9 9.6 %copy-start.24 = (f32[4,1024]{1,0:T(4,128)}, f32[4,1024]{1,0:T(4,128)S(1)}, u32[]{:S(2)}) copy-start(f32[4,1024]{1,0:T(4,128)S(1)} %psum.7) | copy-start | bytes 49156
  821.7 6.9 copy-start.23
  821.7 6.9 copy-start.27
  821.7 6.9 copy-start.32
  821.7 8.2 copy-start.8
  821.7 8.2 copy-start.14
  821.7 8.1 copy-start.34
Sparse Core Ops, SparseCore 0:
  24.8 47.1 all-gather.6
  74.4 27.0 all-gather.8
  128.5 76.6 reduce-scatter.6
  207.8 37.4 all-gather.12
  247.3 45.6 all-gather.10
  294.5 44.6 all-gather.14
  359.3 75.5 reduce-scatter.10
  437.2 77.2 reduce-scatter.8
  519.4 46.3 all-gather.16
  569.6 69.8 reduce-scatter.16
  642.9 51.3 reduce-scatter.14
  696.5 76.8 reduce-scatter.12
where the time goes:
time: 847 us; the launch traced here: 838 us
  waiting for transfers between devices  558 us (66%)
  matrix products  91.1 us (11%)
  local copies, waits for them, and re-layouts  63.6 us (8%)
  other arithmetic  62.1 us (7%)
  blocking collectives  39.9 us (5%)
  between operations  15.2 us (2%)
    reduce_scatter x1, waiting for transfers between devices, local(): lax.psum_scatter(dot_last(activated, ffn_half[1]) * scale_f, 'tensor', sc...  77.4 us
    reduce_scatter x1, waiting for transfers between devices, local(): lax.psum_scatter(dot_last(attended, attn_half[3]) * out_scale, 'tensor',...  74.7 us
    reduce_scatter x1, waiting for transfers between devices, local(): lax.psum_scatter(jnp.einsum('cgj,cdj->gd', d_proj, attn_half[:3], preferr...  70 us
    reduce_scatter x1, waiting for transfers between devices, local(): lax.psum_scatter(dot_last(d_hidden, ffn_half[0]) * scale_d, 'tensor', sca...  68.6 us
    all_gather x1, waiting for transfers between devices, local(): lax.all_gather(h_two_f.astype(jnp.bfloat16), 'tensor', axis=0, tiled=True)  47.8 us
    all_gather x1, waiting for transfers between devices, local(): lax.all_gather(h_one_f.astype(jnp.bfloat16), 'tensor', axis=0, tiled=True)  44.9 us
    psum x1, blocking collectives, local(): lax.psum(jnp.stack([d_gain_one, d_bias_one, d_gain_two, d_bias_two]), ('d...  39.9 us
    reduce_scatter x1, waiting for transfers between devices, local(): lax.psum_scatter(attn_part, 'dp', scatter_dimension=1, tiled=True)  39 us
  transfers between devices with their start and end apart: 12, of which 12 were waited for; matrix products, arithmetic and copies ran while one was open for 15% of the time, Pallas kernels for 0%

commit v1 on v0

--- a/solution.py
+++ b/solution.py
@@ -1,6 +1,9 @@
 import jax
 import jax.numpy as jnp
+import numpy as np
 from jax import lax
+from jax.experimental import pallas as pl
+from jax.experimental.pallas import tpu as pltpu
 from jax.sharding import PartitionSpec as P
 
 HD = 64
@@ -252,6 +255,929 @@
     )
 
 
+MESH = pl.DeviceIdType.MESH
+TOK = 256
+CHUNK = 32
+PIECES = ("qkv", "out", "up", "down")
+
+
+def contract(left, right, left_dim, right_dim):
+    return lax.dot_general(
+        left,
+        right,
+        (((left_dim,), (right_dim,)), ((), ())),
+        preferred_element_type=jnp.float32,
+    )
+
+
+def flip(bit):
+    return 1 - bit
+
+
+def aligned(start, size):
+    return pl.ds(pl.multiple_of(start, size), size)
+
+
+def sin_cos(angle, odd):
+    turns = jnp.floor(angle * (2.0 / np.pi) + 0.5)
+    rest = angle - turns * 1.5703125
+    rest = rest - turns * 4.837512969970703125e-4
+    rest = rest - turns * 7.54978995489188216e-8
+    quadrant = turns.astype(jnp.int32) + odd
+    square = rest * rest
+    sine = ((-1.9515295891e-4 * square + 8.3321608736e-3) * square - 1.6666654611e-1) * square
+    sine = sine * rest + rest
+    cosine = (2.443315711809948e-5 * square - 1.388731625493765e-3) * square
+    cosine = (cosine + 4.166664568298827e-2) * square * square - 0.5 * square + 1.0
+    value = jnp.where((quadrant & 1) == 1, cosine, sine)
+    return jnp.where((quadrant & 2) == 2, -value, value)
+
+
+def normalized(rows):
+    centred = rows - jnp.mean(rows, axis=-1, keepdims=True)
+    spread = lax.rsqrt(jnp.mean(centred * centred, axis=-1, keepdims=True) + norm_eps)
+    return centred * spread, spread
+
+
+def fold_rows(values):
+    total = values[0:8]
+    for first in range(8, values.shape[0], 8):
+        total = total + values[first : first + 8]
+    return total
+
+
+def block_kernel(
+    tok_in,
+    cot_in,
+    info_in,
+    attn_in,
+    ffn_in,
+    norm_in,
+    freq_in,
+    tok_out,
+    grad_out,
+    attn_parts,
+    ffn_parts,
+    norm_out,
+    info,
+    tok_buf,
+    g_all,
+    cols,
+    seg_col,
+    x_embed,
+    x_mid,
+    d_mid,
+    h_one,
+    h_two,
+    d_mid_all,
+    attn_w,
+    ffn_w,
+    qkv,
+    prob,
+    att,
+    d_att,
+    act,
+    d_hid,
+    send_a,
+    send_b,
+    recv_a,
+    recv_b,
+    acc_a,
+    acc_b,
+    d_qkv,
+    kv_send,
+    kv_recv,
+    dk_tmp,
+    dv_tmp,
+    ffn_sum,
+    attn_stage,
+    attn_sum,
+    ffn_box,
+    attn_box,
+    norm_acc,
+    norm_recv,
+    one_send,
+    one_recv,
+    two_send,
+    two_recv,
+    sib_send,
+    sib_recv,
+    act_send,
+    act_recv,
+    grad_sib_send,
+    grad_sib_recv,
+    grad_box_send,
+    grad_box_recv,
+    grad_own_send,
+    grad_own_recv,
+    norm_send_sem,
+    norm_recv_sem,
+):
+    width = freq_in.shape[1]
+    scale_d = width ** (-0.5)
+    scale_f = FF ** (-0.5)
+    out_scale = out_gain * scale_d
+    score_scale = HD ** (-0.5)
+
+    d = lax.axis_index("dp")
+    t = lax.axis_index("tensor")
+    core = lax.rem(d, 2)
+    col = lax.div(d, 2)
+    x_bit = lax.rem(col, 2)
+    y_bit = lax.div(col, 2)
+    par = lax.rem(t, 2)
+    half = lax.div(t, 2)
+    quarter = 2 * par + core
+    home = core == half
+    d_sib = d + 1 - 2 * core
+    d_x = d + 2 - 4 * x_bit
+    d_y = d + 4 - 8 * y_bit
+    d_xy = d_x + 4 - 8 * y_bit
+    t_pair = t + 1 - 2 * par
+    t_far = t + 2 - 4 * half
+    sib = (d_sib, t)
+    pair = (d, t_pair)
+    swap = (d_sib, t_far)
+    nears = ((d_x, t), (d_y, t), (d_xy, t))
+    near_cols = (lax.div(d_x, 2), lax.div(d_y, 2), lax.div(d_xy, 2))
+
+    def remote(src, dst, send, recv, device):
+        return pltpu.make_async_remote_copy(
+            src_ref=src, dst_ref=dst, send_sem=send, recv_sem=recv, device_id=device, device_id_type=MESH
+        )
+
+    barrier = pltpu.get_barrier_semaphore()
+    peers = list(nears)
+    for dd in (d, d_sib):
+        for tt in (t, t_pair, t_far, t_pair + t_far - t):
+            peers.append((dd, tt))
+    peers = peers[:3] + peers[4:]
+    for peer in peers:
+        pl.semaphore_signal(barrier, inc=1, device_id=peer, device_id_type=MESH)
+    pl.semaphore_wait(barrier, len(peers))
+
+    own = aligned(par * TOK, TOK)
+    other = aligned(flip(par) * TOK, TOK)
+
+    def swap_in(src, dst, index):
+        @pl.when(home)
+        def _():
+            pltpu.make_async_copy(src, dst, act_recv.at[index]).start()
+
+        @pl.when(jnp.logical_not(home))
+        def _():
+            remote(src, dst, act_send.at[index], act_recv.at[index], swap).start()
+
+    def swap_wait(src, dst, index):
+        pltpu.make_async_copy(src, dst, act_recv.at[index]).wait()
+
+    def swap_sent(src, dst, index):
+        @pl.when(jnp.logical_not(home))
+        def _():
+            remote(src, dst, act_send.at[index], act_recv.at[index], swap).wait_send()
+
+    def piece_view(piece, h, rows):
+        if piece == 0:
+            return attn_w.at[h, 0:3, rows, :]
+        if piece == 1:
+            return attn_w.at[h, 3, rows, :]
+        return ffn_w.at[h, piece - 2, rows, :]
+
+    def piece_source(piece):
+        if piece == 0:
+            return attn_in.at[0:3]
+        if piece == 1:
+            return attn_in.at[3]
+        return ffn_in.at[piece - 2]
+
+    def one_copy(piece, k):
+        dst = piece_view(piece, par, aligned(d * 128, 128))
+        target = (d - core + par, half + 2 * k)
+        return remote(
+            piece_source(piece), dst, one_send.at[piece, k], one_recv.at[piece, core], target
+        )
+
+    def one_is_own(k):
+        if k == 0:
+            return jnp.logical_and(core == par, t == half)
+        return jnp.logical_and(core == par, t == half + 2)
+
+    def one_start(piece):
+        for k in range(2):
+
+            @pl.when(one_is_own(k))
+            def _():
+                dst = piece_view(piece, par, aligned(d * 128, 128))
+                pltpu.make_async_copy(piece_source(piece), dst, one_recv.at[piece, core]).start()
+
+            @pl.when(jnp.logical_not(one_is_own(k)))
+            def _():
+                one_copy(piece, k).start()
+
+    def one_sent(piece):
+        for k in range(2):
+
+            @pl.when(jnp.logical_not(one_is_own(k)))
+            def _():
+                one_copy(piece, k).wait_send()
+
+    def two_copy(piece, k):
+        view = piece_view(piece, core, aligned(col * 256, 256))
+        return remote(view, view, two_send.at[piece, k], two_recv.at[piece, k], nears[k])
+
+    def sib_copy(piece, k):
+        which = col if k == 0 else near_cols[k - 1]
+        view = piece_view(piece, core, aligned(which * 256, 256))
+        return remote(view, view, sib_send.at[piece, k], sib_recv.at[piece, k], sib)
+
+    def spread(piece):
+        for c0 in range(2):
+            rows = aligned((2 * col + c0) * 128, 128)
+            pltpu.make_async_copy(
+                piece_source(piece), piece_view(piece, core, rows), one_recv.at[piece, c0]
+            ).wait()
+        for k in range(3):
+            two_copy(piece, k).start()
+        sib_copy(piece, 0).start()
+
+    def relay(piece):
+        for k in range(3):
+            two_copy(piece, k).wait_recv()
+            sib_copy(piece, k + 1).start()
+
+    def ready(piece):
+        for k in range(4):
+            sib_copy(piece, k).wait_recv()
+
+    def sent(piece):
+        for k in range(3):
+            two_copy(piece, k).wait_send()
+        for k in range(4):
+            sib_copy(piece, k).wait_send()
+
+    swap_in(info_in, info, 0)
+    one_start(0)
+    swap_in(tok_in, tok_buf, 1)
+    swap_wait(info_in, info, 0)
+
+    seg_first = (2 * core + par) * TOK
+    seg_mine = info[0:1, aligned(seg_first, TOK)]
+    flags = jnp.zeros_like(seg_mine)
+    for item in range(4):
+        flags = flags + jnp.where(seg_mine == item, info[2:3, item : item + 1], 0)
+
+    def as_column(row):
+        row = row.astype(jnp.float32)
+        return jnp.transpose(jnp.broadcast_to(row, (128, row.shape[1])))
+
+    cols[0] = as_column(info[1:2, 0:TOK])
+    cols[1] = as_column(flags)
+    seg_col[...] = as_column(info[0:1, aligned(core * 512, 512)])
+    seg_row = info[0:1, :].astype(jnp.float32)
+    odd = lax.rem(lax.broadcasted_iota(jnp.int32, (1, width), 1), 2)
+
+    def encode(step, carry):
+        rows = aligned(step * CHUNK, CHUNK)
+        angle = cols[0, rows, 0:1] * freq_in[0:1, :]
+        x_embed[rows, :] = cols[1, rows, 0:1] * sin_cos(angle, odd)
+        return carry
+
+    lax.fori_loop(0, TOK // CHUNK, encode, 0)
+
+    spread(0)
+    one_start(1)
+    swap_in(cot_in, g_all.at[own, :], 2)
+    one_start(2)
+    one_start(3)
+    swap_wait(tok_in, tok_buf, 1)
+
+    def norm_first(step, carry):
+        rows = aligned(step * CHUNK, CHUNK)
+        value = x_embed[rows, :] + tok_buf[rows, :].astype(jnp.float32)
+        x_embed[rows, :] = value
+        unit, _ = normalized(value)
+        row = aligned(par * TOK + step * CHUNK, CHUNK)
+        h_one[row, :] = (unit * norm_in[0:1, :] + norm_in[1:2, :]).astype(jnp.bfloat16)
+        return carry
+
+    lax.fori_loop(0, TOK // CHUNK, norm_first, 0)
+
+    def pair_copy(buf, index):
+        return remote(buf.at[own, :], buf.at[own, :], act_send.at[index], act_recv.at[index], pair)
+
+    pair_copy(h_one, 3).start()
+    relay(0)
+    spread(1)
+    ready(0)
+    swap_wait(cot_in, g_all.at[own, :], 2)
+    pair_copy(g_all, 4).start()
+    spread(2)
+
+    def project(first):
+        rows = aligned(first * TOK, TOK)
+        where = aligned(core * 512 + first * TOK, TOK)
+
+        def step(i, carry):
+            h = lax.div(i, 3)
+            m = lax.rem(i, 3)
+            out = contract(h_one[rows, :], attn_w[h, m], 1, 0) * scale_d
+            qkv[m, h, where, :] = out.astype(jnp.bfloat16)
+            return carry
+
+        lax.fori_loop(0, 6, step, 0)
+
+    def kv_copy(first, index):
+        view = qkv.at[1:3, :, aligned(core * 512 + first * TOK, TOK), :]
+        return remote(view, view, act_send.at[index], act_recv.at[index], sib)
+
+    project(par)
+    kv_copy(par, 5).start()
+    pair_copy(h_one, 3).wait_recv()
+    project(flip(par))
+    kv_copy(flip(par), 6).start()
+    relay(1)
+    spread(3)
+    kv_copy(par, 5).wait_recv()
+    kv_copy(flip(par), 6).wait_recv()
+
+    lane_half = lax.broadcasted_iota(jnp.int32, (TOK, 128), 1)
+    lane_masks = (lane_half < HD, lane_half >= HD)
+
+    def attend(i, carry):
+        jj = lax.div(i, 2)
+        rows = aligned(lax.rem(i, 2) * TOK, TOK)
+        q_rows = aligned(core * 512 + lax.rem(i, 2) * TOK, TOK)
+        h = lax.div(jj, 2)
+        lanes = aligned(lax.rem(jj, 2) * 128, 128)
+        queries = qkv[0, h, q_rows, lanes] * jnp.bfloat16(score_scale)
+        keys = qkv[1, h, :, lanes]
+        vals = qkv[2, h, :, lanes]
+        allowed = seg_col[rows, 0:1] == seg_row
+        outs = []
+        for a in range(2):
+            query = jnp.where(lane_masks[a], queries, jnp.bfloat16(0))
+            scores = jnp.where(allowed, contract(query, keys, 1, 1), masked_score)
+            top = jnp.max(scores, axis=1, keepdims=True)
+            weight = jnp.exp(scores - top)
+            total = jnp.sum(weight, axis=1, keepdims=True)
+            share = (weight * (1.0 / total)).astype(jnp.bfloat16)
+            prob[2 * jj + a, rows, :] = share
+            outs.append(contract(share, vals, 1, 0))
+        att[h, rows, lanes] = jnp.where(lane_masks[0], outs[0], outs[1]).astype(jnp.bfloat16)
+        return carry
+
+    lax.fori_loop(0, 8, attend, 0)
+
+    ready(1)
+    relay(2)
+
+    def split_product(product, scale, send_buf, recv_buf, acc, index, steps):
+        def step_send(n, carry):
+            lanes = aligned(n * TOK, TOK)
+            send_buf[:, lanes] = (product(other, n) * scale).astype(jnp.bfloat16)
+            return carry
+
+        lax.fori_loop(0, steps, step_send, 0)
+        remote(send_buf, recv_buf, act_send.at[index], act_recv.at[index], pair).start()
+
+        def step_keep(n, carry):
+            lanes = aligned(n * TOK, TOK)
+            acc[:, lanes] = product(own, n) * scale
+            return carry
+
+        lax.fori_loop(0, steps, step_keep, 0)
+
+    def split_wait(send_buf, recv_buf, index):
+        remote(send_buf, recv_buf, act_send.at[index], act_recv.at[index], pair).wait()
+
+    def out_product(rows, n):
+        outs = aligned(n * TOK, TOK)
+        total = contract(att[0, rows, :], attn_w[0, 3, outs, :], 1, 1)
+        return total + contract(att[1, rows, :], attn_w[1, 3, outs, :], 1, 1)
+
+    split_product(out_product, out_scale, send_a, recv_a, acc_a, 7, 4)
+    relay(3)
+    split_wait(send_a, recv_a, 7)
+
+    def norm_second(step, carry):
+        rows = aligned(step * CHUNK, CHUNK)
+        value = x_embed[rows, :] + (acc_a[rows, :] + recv_a[rows, :].astype(jnp.float32))
+        x_mid[rows, :] = value
+        unit, _ = normalized(value)
+        row = aligned(par * TOK + step * CHUNK, CHUNK)
+        h_two[row, :] = (unit * norm_in[2:3, :] + norm_in[3:4, :]).astype(jnp.bfloat16)
+        return carry
+
+    lax.fori_loop(0, TOK // CHUNK, norm_second, 0)
+    pair_copy(h_two, 8).start()
+    pair_copy(g_all, 4).wait_recv()
+    ready(2)
+    ready(3)
+
+    def feed(first):
+        rows = aligned(first * TOK, TOK)
+
+        def step(i, carry):
+            h = lax.div(i, 4)
+            lanes = aligned(lax.rem(i, 4) * 256, 256)
+            hidden = contract(h_two[rows, :], ffn_w[h, 0, :, lanes], 1, 0) * scale_d
+            d_act = contract(g_all[rows, :], ffn_w[h, 1, :, lanes], 1, 0) * scale_f
+            gate = 0.5 + 0.5 * lax.erf(hidden * np.float32(np.sqrt(0.5)))
+            act[h, rows, lanes] = (hidden * gate).astype(jnp.bfloat16)
+            bell = jnp.exp(-0.5 * hidden * hidden) * np.float32(1.0 / np.sqrt(2.0 * np.pi))
+            d_hid[h, rows, lanes] = (d_act * (gate + hidden * bell)).astype(jnp.bfloat16)
+            return carry
+
+        lax.fori_loop(0, 8, step, 0)
+
+    feed(par)
+    pair_copy(h_two, 8).wait_recv()
+    feed(flip(par))
+
+    def hid_product(rows, n):
+        outs = aligned(n * TOK, TOK)
+        total = contract(d_hid[0, rows, :], ffn_w[0, 0, outs, :], 1, 1)
+        return total + contract(d_hid[1, rows, :], ffn_w[1, 0, outs, :], 1, 1)
+
+    split_product(hid_product, scale_d, send_a, recv_a, acc_a, 9, 4)
+
+    def down_product(rows, n):
+        outs = aligned(n * TOK, TOK)
+        total = contract(act[0, rows, :], ffn_w[0, 1, outs, :], 1, 1)
+        return total + contract(act[1, rows, :], ffn_w[1, 1, outs, :], 1, 1)
+
+    split_product(down_product, scale_f, send_b, recv_b, acc_b, 10, 4)
+    for piece in range(4):
+        one_sent(piece)
+        sent(piece)
+
+    def grad_tile(kind, m, h, tile):
+        cells = aligned(tile * 256, 256)
+        if kind == 0:
+            left = h_one[:, cells] if m < 3 else d_mid_all[:, cells]
+            right = d_qkv[m, h] if m < 3 else att[h]
+            return contract(left, right, 0, 0) * (scale_d if m < 3 else out_scale)
+        left = h_two[:, cells] if m == 0 else g_all[:, cells]
+        right = d_hid[h] if m == 0 else act[h]
+        return contract(left, right, 0, 0) * (scale_d if m == 0 else scale_f)
+
+    def stage_view(kind, m, rows):
+        return attn_stage.at[m, rows, :] if kind == 0 else ffn_w.at[0, m, rows, :]
+
+    def sum_view(kind, m, rows):
+        return attn_sum.at[m, rows, :] if kind == 0 else ffn_sum.at[m, rows, :]
+
+    def slot(kind, m):
+        return m if kind == 0 else 4 + m
+
+    def tile_copy(kind, m, tile):
+        rows = aligned(tile * 256, 256)
+        index = slot(kind, m)
+        return remote(
+            stage_view(kind, m, rows),
+            sum_view(kind, m, rows),
+            grad_sib_send.at[index, tile],
+            grad_sib_recv.at[index, tile],
+            sib,
+        )
+
+    def grads_sibling(kind, m):
+        def step(tile, carry):
+            rows = aligned(tile * 256, 256)
+            stage = stage_view(kind, m, rows)
+            stage[...] = grad_tile(kind, m, flip(core), tile).astype(jnp.bfloat16)
+            tile_copy(kind, m, tile).start()
+            return carry
+
+        lax.fori_loop(0, 4, step, 0)
+
+    def tile_place(k):
+        to_x = 1 - lax.div(k, 2)
+        to_y = 1 - lax.rem(k, 2)
+        x_new = x_bit + to_x - 2 * x_bit * to_x
+        y_new = y_bit + to_y - 2 * y_bit * to_y
+        return 2 * y_new + x_new
+
+    def box_view(kind, m, k):
+        return attn_box.at[k, m] if kind == 0 else ffn_box.at[k, m]
+
+    def box_copy(kind, m, k):
+        place = tile_place(k)
+        index = slot(kind, m)
+        return remote(
+            sum_view(kind, m, aligned(place * 256, 256)),
+            box_view(kind, m, k),
+            grad_box_send.at[index, k],
+            grad_box_recv.at[index, k],
+            (2 * place + core, t),
+        )
+
+    def grads_own(kind, m):
+        def step(k, carry):
+            place = tile_place(k)
+            total = grad_tile(kind, m, core, place)
+            tile_copy(kind, m, place).wait_recv()
+            view = sum_view(kind, m, aligned(place * 256, 256))
+            view[...] = (total + view[...].astype(jnp.float32)).astype(jnp.bfloat16)
+
+            @pl.when(k < 3)
+            def _():
+                box_copy(kind, m, k).start()
+
+            return carry
+
+        lax.fori_loop(0, 4, step, 0)
+
+    def own_copy(kind, m, c0):
+        rows = aligned(col * 256 + c0 * 128, 128)
+        dst = attn_parts.at[half, m] if kind == 0 else ffn_parts.at[half, m]
+        index = slot(kind, m)
+        return remote(
+            sum_view(kind, m, rows),
+            dst,
+            grad_own_send.at[index, c0],
+            grad_own_recv.at[index, half],
+            (d - core + c0, quarter),
+        )
+
+    def own_is_here(c0):
+        return jnp.logical_and(core == c0, t == quarter)
+
+    def grads_columns(kind, m):
+        for k in range(3):
+            box_copy(kind, m, k).wait_recv()
+
+        def step(i, carry):
+            rows = aligned(col * 256 + i * CHUNK, CHUNK)
+            part = aligned(i * CHUNK, CHUNK)
+            view = sum_view(kind, m, rows)
+            total = view[...].astype(jnp.float32)
+            for k in range(3):
+                total = total + box_view(kind, m, k)[part, :].astype(jnp.float32)
+            view[...] = total.astype(jnp.bfloat16)
+            return carry
+
+        lax.fori_loop(0, 256 // CHUNK, step, 0)
+        for c0 in range(2):
+
+            @pl.when(own_is_here(c0))
+            def _():
+                rows = aligned(col * 256 + c0 * 128, 128)
+                dst = attn_parts.at[half, m] if kind == 0 else ffn_parts.at[half, m]
+                pltpu.make_async_copy(
+                    sum_view(kind, m, rows), dst, grad_own_recv.at[slot(kind, m), half]
+                ).start()
+
+            @pl.when(jnp.logical_not(own_is_here(c0)))
+            def _():
+                own_copy(kind, m, c0).start()
+
+    def grads_finish(kind, m):
+        index = slot(kind, m)
+        for k in range(2):
+            src = sum_view(kind, m, aligned(col * 256, 128))
+            dst = attn_parts.at[k, m] if kind == 0 else ffn_parts.at[k, m]
+            pltpu.make_async_copy(src, dst, grad_own_recv.at[index, k]).wait()
+        for k in range(4):
+            tile_copy(kind, m, k).wait_send()
+        for k in range(3):
+            box_copy(kind, m, k).wait_send()
+        for c0 in range(2):
+
+            @pl.when(jnp.logical_not(own_is_here(c0)))
+            def _():
+                own_copy(kind, m, c0).wait_send()
+
+    grads_sibling(1, 0)
+    grads_sibling(1, 1)
+
+    split_wait(send_a, recv_a, 9)
+
+    def back_norm(step, base, gain, add, acc, out):
+        rows = aligned(step * CHUNK, CHUNK)
+        unit, spread_row = normalized(base[rows, :])
+        d_rows = acc[rows, :] + recv_a[rows, :].astype(jnp.float32)
+        scaled = d_rows * gain
+        inner = jnp.mean(scaled * unit, axis=-1, keepdims=True)
+        result = add + spread_row * (scaled - jnp.mean(scaled, axis=-1, keepdims=True) - unit * inner)
+        out(rows, result)
+        return fold_rows(d_rows * unit), fold_rows(d_rows)
+
+    def back_second(step, carry):
+        def out(rows, result):
+            d_mid[rows, :] = result
+            row = aligned(par * TOK + step * CHUNK, CHUNK)
+            d_mid_all[row, :] = result.astype(jnp.bfloat16)
+
+        row = aligned(par * TOK + step * CHUNK, CHUNK)
+        add = g_all[row, :].astype(jnp.float32)
+        d_gain, d_bias = back_norm(step, x_mid, norm_in[2:3, :], add, acc_a, out)
+        norm_acc[2] = norm_acc[2] + d_gain
+        norm_acc[3] = norm_acc[3] + d_bias
+        return carry
+
+    norm_acc[...] = jnp.zeros_like(norm_acc)
+    lax.fori_loop(0, TOK // CHUNK, back_second, 0)
+    pair_copy(d_mid_all, 11).start()
+
+    grads_own(1, 0)
+    grads_own(1, 1)
+
+    split_wait(send_b, recv_b, 10)
+
+    def finish_out(step, carry):
+        rows = aligned(step * CHUNK, CHUNK)
+        total = x_mid[rows, :] + (acc_b[rows, :] + recv_b[rows, :].astype(jnp.float32))
+        tok_buf[rows, :] = total.astype(jnp.bfloat16)
+        return carry
+
+    lax.fori_loop(0, TOK // CHUNK, finish_out, 0)
+    swap_in(tok_buf, tok_out, 12)
+
+    def back_out(first):
+        rows = aligned(first * TOK, TOK)
+
+        def step(h, carry):
+            out = contract(d_mid_all[rows, :], attn_w[h, 3], 1, 0) * out_scale
+            d_att[h, rows, :] = out.astype(jnp.bfloat16)
+            return carry
+
+        lax.fori_loop(0, 2, step, 0)
+
+    back_out(par)
+    pair_copy(d_mid_all, 11).wait_recv()
+    back_out(flip(par))
+    grads_sibling(0, 3)
+
+    def attend_back(jj, carry):
+        h = lax.div(jj, 2)
+        lanes = aligned(lax.rem(jj, 2) * 128, 128)
+        keys = qkv[1, h, :, lanes]
+        vals = qkv[2, h, :, lanes]
+        dk_total = None
+        dv_total = None
+        for part in range(2):
+            rows = pl.ds(part * TOK, TOK)
+            q_rows = aligned(core * 512 + part * TOK, TOK)
+            queries = qkv[0, h, q_rows, lanes] * jnp.bfloat16(score_scale)
+            d_outs = d_att[h, rows, lanes]
+            inner = d_outs.astype(jnp.float32) * att[h, rows, lanes].astype(jnp.float32)
+            dqs = []
+            for a in range(2):
+                share = prob[2 * jj + a, rows, :]
+                d_out = jnp.where(lane_masks[a], d_outs, jnp.bfloat16(0))
+                query = jnp.where(lane_masks[a], queries, jnp.bfloat16(0))
+                row_sum = jnp.sum(jnp.where(lane_masks[a], inner, 0.0), axis=1, keepdims=True)
+                d_prob = contract(d_out, vals, 1, 1)
+                d_score = (share.astype(jnp.float32) * (d_prob - row_sum)).astype(jnp.bfloat16)
+                dqs.append(contract(d_score, keys, 1, 0))
+                dk = contract(query, d_score, 0, 0)
+                dv = contract(d_out, share, 0, 0)
+                dk_total = dk if dk_total is None else dk_total + dk
+                dv_total = dv if dv_total is None else dv_total + dv
+            d_query = jnp.where(lane_masks[0], dqs[0], dqs[1]) * score_scale
+            d_qkv[0, h, rows, lanes] = d_query.astype(jnp.bfloat16)
+        dk_tmp[...] = dk_total
+        dv_tmp[...] = dv_total
+        mine = aligned(core * 512, 512)
+        theirs = aligned(flip(core) * 512, 512)
+        d_qkv[1, h, :, lanes] = jnp.transpose(dk_tmp[:, mine]).astype(jnp.bfloat16)
+        d_qkv[2, h, :, lanes] = jnp.transpose(dv_tmp[:, mine]).astype(jnp.bfloat16)
+        kv_send[jj, 0] = jnp.transpose(dk_tmp[:, theirs]).astype(jnp.bfloat16)
+        kv_send[jj, 1] = jnp.transpose(dv_tmp[:, theirs]).astype(jnp.bfloat16)
+        kv_grad_copy(jj).start()
+        return carry
+
+    def kv_grad_copy(jj):
+        return remote(kv_send.at[jj], kv_recv.at[jj], act_send.at[13 + jj], act_recv.at[13 + jj], sib)
+
+    lax.fori_loop(0, 4, attend_back, 0)
+
+    def join_kv(jj, carry):
+        kv_grad_copy(jj).wait()
+        h = lax.div(jj, 2)
+        lanes = aligned(lax.rem(jj, 2) * 128, 128)
+        for m in range(2):
+            total = d_qkv[m + 1, h, :, lanes].astype(jnp.float32) + kv_recv[jj, m].astype(jnp.float32)
+            d_qkv[m + 1, h, :, lanes] = total.astype(jnp.bfloat16)
+        return carry
+
+    grads_columns(1, 0)
+    grads_columns(1, 1)
+    lax.fori_loop(0, 4, join_kv, 0)
+
+    def first_product(rows, n):
+        outs = aligned(n * TOK, TOK)
+        total = None
+        for h in range(2):
+            for m in range(3):
+                part = contract(d_qkv[m, h, rows, :], attn_w[h, m, outs, :], 1, 1)
+                total = part if total is None else total + part
+        return total
+
+    split_product(first_product, scale_d, send_a, recv_a, acc_a, 17, 4)
+    for m in range(3):
+        grads_sibling(0, m)
+    grads_own(0, 3)
+    for m in range(3):
+        grads_own(0, m)
+
+    split_wait(send_a, recv_a, 17)
+    swap_sent(tok_buf, tok_out, 12)
+    swap_wait(tok_buf, tok_out, 12)
+
+    def back_first(step, carry):
+        def out(rows, result):
+            tok_buf[rows, :] = result.astype(jnp.bfloat16)
+
+        add = d_mid[aligned(step * CHUNK, CHUNK), :]
+        d_gain, d_bias = back_norm(step, x_embed, norm_in[0:1, :], add, acc_a, out)
+        norm_acc[0] = norm_acc[0] + d_gain
+        norm_acc[1] = norm_acc[1] + d_bias
+        return carry
+
+    lax.fori_loop(0, TOK // CHUNK, back_first, 0)
+    swap_in(tok_buf, grad_out, 18)
+
+    for row in range(4):
+        norm_out[row : row + 1, :] = jnp.sum(norm_acc[row], axis=0, keepdims=True)
+    norm_out[4:8, :] = jnp.zeros((4, width), jnp.float32)
+    for i, peer in enumerate((sib, nears[0], nears[1], pair, (d, t_far))):
+        copy = remote(norm_out, norm_recv.at[i], norm_send_sem.at[i], norm_recv_sem.at[i], peer)
+        copy.start()
+        copy.wait()
+        norm_out[...] = norm_out[...] + norm_recv[i]
+
+    for m in (3, 0, 1, 2):
+        grads_columns(0, m)
+    for m in range(2):
+        grads_finish(1, m)
+    for m in range(4):
+        grads_finish(0, m)
+    swap_sent(tok_buf, grad_out, 18)
+    swap_wait(tok_buf, grad_out, 18)
+    swap_sent(info_in, info, 0)
+    swap_sent(tok_in, tok_buf, 1)
+    swap_sent(cot_in, g_all.at[own, :], 2)
+    pair_copy(h_one, 3).wait_send()
+    pair_copy(g_all, 4).wait_send()
+    pair_copy(h_two, 8).wait_send()
+    pair_copy(d_mid_all, 11).wait_send()
+    kv_copy(par, 5).wait_send()
+    kv_copy(flip(par), 6).wait_send()
+
+
+def run_block(tok, cot, info, attn_half, ffn_half, norm_weight, freqs):
+    bf16, f32 = jnp.bfloat16, jnp.float32
+    vmem, sem = pltpu.VMEM, pltpu.SemaphoreType.DMA
+    width = tok.shape[1]
+    wide, ff_q, head_q = 2 * TOK, ffn_half.shape[2], attn_half.shape[2]
+    group = info.shape[1]
+    hbm = pl.BlockSpec(memory_space=pl.ANY)
+    on_chip = pl.BlockSpec(memory_space=pltpu.VMEM)
+    return pl.pallas_call(
+        block_kernel,
+        out_shape=(
+            jax.ShapeDtypeStruct(tok.shape, bf16),
+            jax.ShapeDtypeStruct(tok.shape, bf16),
+            jax.ShapeDtypeStruct((2,) + attn_half.shape, bf16),
+            jax.ShapeDtypeStruct((2,) + ffn_half.shape, bf16),
+            jax.ShapeDtypeStruct((8, width), f32),
+        ),
+        in_specs=[hbm, hbm, hbm, hbm, hbm, on_chip, on_chip],
+        out_specs=(hbm, hbm, hbm, hbm, on_chip),
+        scratch_shapes=[
+            vmem((8, group), jnp.int32),
+            vmem((TOK, width), bf16),
+            vmem((wide, width), bf16),
+            vmem((2, TOK, 128), f32),
+            vmem((wide, 128), f32),
+            vmem((TOK, width), f32),
+            vmem((TOK, width), f32),
+            vmem((TOK, width), f32),
+            vmem((wide, width), bf16),
+            vmem((wide, width), bf16),
+            vmem((wide, width), bf16),
+            vmem((2, 4, width, head_q), bf16),
+            vmem((2, 2, width, ff_q), bf16),
+            vmem((3, 2, group, head_q), bf16),
+            vmem((8, wide, group), bf16),
+            vmem((2, wide, head_q), bf16),
+            vmem((2, wide, head_q), bf16),
+            vmem((2, wide, ff_q), bf16),
+            vmem((2, wide, ff_q), bf16),
+            vmem((TOK, width), bf16),
+            vmem((TOK, width), bf16),
+            vmem((TOK, width), bf16),
+            vmem((TOK, width), bf16),
+            vmem((TOK, width), f32),
+            vmem((TOK, width), f32),
+            vmem((3, 2, wide, head_q), bf16),
+            vmem((4, 2, wide, 128), bf16),
+            vmem((4, 2, wide, 128), bf16),
+            vmem((128, group), f32),
+            vmem((128, group), f32),
+            vmem((2, width, ff_q), bf16),
+            vmem((4, width, head_q), bf16),
+            vmem((4, width, head_q), bf16),
+            vmem((3, 2, 256, ff_q), bf16),
+            vmem((3, 4, 256, head_q), bf16),
+            vmem((4, 8, width), f32),
+            vmem((5, 8, width), f32),
+            sem((4, 2)),
+            sem((4, 2)),
+            sem((4, 3)),
+            sem((4, 3)),
+            sem((4, 4)),
+            sem((4, 4)),
+            sem((19,)),
+            sem((19,)),
+            sem((6, 4)),
+            sem((6, 4)),
+            sem((6, 3)),
+            sem((6, 3)),
+            sem((6, 2)),
+            sem((6, 2)),
+            sem((5,)),
+            sem((5,)),
+        ],
+        compiler_params=pltpu.CompilerParams(
+            collective_id=0, has_side_effects=True, vmem_limit_bytes=VMEM_LIMIT
+        ),
+        cost_estimate=pl.CostEstimate(
+            flops=30_000_000_000, bytes_accessed=30_000_000, transcendentals=10_000_000
+        ),
+        name="block",
+    )(tok, cot, info, attn_half, ffn_half, norm_weight, freqs)
+
+
+VMEM_LIMIT = 63 * 2**20
+
+
+def local_fast(
+    tokens,
+    cotangent,
+    positions,
+    segment_ids,
+    spatial_flag,
+    attn_weight,
+    attn_moments,
+    attn_ema,
+    ffn_weight,
+    ffn_moments,
+    ffn_ema,
+    norm_weight,
+    norm_moments,
+    norm_ema,
+):
+    width = tokens.shape[1]
+    group = segment_ids.shape[1]
+    exponent = -2.0 * (np.arange(width) // 2) / width
+    freqs = jnp.asarray(np.tile((10000.0**exponent).astype(np.float32), (8, 1)))
+    info = jnp.zeros((8, group), jnp.int32)
+    info = info.at[0].set(segment_ids[0])
+    info = info.at[1, : positions.shape[1]].set(positions[0])
+    info = info.at[2, : spatial_flag.shape[1]].set(spatial_flag[0])
+    grad_scale = float(group * lax.axis_size("dp")) ** (-0.5)
+    out_tokens, grad_tokens, attn_parts, ffn_parts, norm_rows = run_block(
+        tokens,
+        cotangent,
+        info,
+        attn_weight.astype(jnp.bfloat16),
+        ffn_weight.astype(jnp.bfloat16),
+        norm_weight,
+        freqs,
+    )
+    attn_grad = attn_parts[0].astype(jnp.float32) + attn_parts[1].astype(jnp.float32)
+    ffn_grad = ffn_parts[0].astype(jnp.float32) + ffn_parts[1].astype(jnp.float32)
+    norm_grad = norm_rows[:4]
+    attn_new, attn_mom_new, attn_ema_new = adam_update(
+        attn_weight, attn_moments, attn_ema, attn_grad * grad_scale
+    )
+    ffn_new, ffn_mom_new, ffn_ema_new = adam_update(
+        ffn_weight, ffn_moments, ffn_ema, ffn_grad * grad_scale
+    )
+    norm_new, norm_mom_new, norm_ema_new = adam_update(
+        norm_weight, norm_moments, norm_ema, norm_grad * grad_scale
+    )
+    return (
+        out_tokens,
+        grad_tokens,
+        attn_grad,
+        ffn_grad,
+        norm_grad,
+        attn_new,
+        attn_mom_new,
+        attn_ema_new,
+        ffn_new,
+        ffn_mom_new,
+        ffn_ema_new,
+        norm_new,
+        norm_mom_new,
+        norm_ema_new,
+    )
+
+
 def solution(mesh):
     placed = (
         P(("dp", "tensor"), None),
@@ -269,8 +1195,9 @@
         P(),
         P(),
     )
+    fast = mesh.shape["dp"] == 8 and mesh.shape["tensor"] == 4
     return jax.shard_map(
-        local,
+        local_fast if fast else local,
         mesh=mesh,
         in_specs=placed,
         out_specs=(

time: 847 us -> 263 us (0.31)
  waiting for transfers between devices: 558 us -> 0 us
  Pallas kernels: 0 us -> 240 us
  matrix products: 91.1 us -> 0 us
  local copies, waits for them, and re-layouts: 63.6 us -> 4.67 us
  other arithmetic: 62.1 us -> 15.2 us
  blocking collectives: 39.9 us -> 0 us
  between operations: 15.2 us -> 0.8 us
    reduce_scatter x6 -> x0, waiting for transfers between devices: 338 us -> none  [the longest x1 77.4 us: local(): lax.psum_scatter(dot_last(activated, ffn_half[1]) * scale_f, 'tensor', sc...]
    pallas_call x0 -> x1, Pallas kernels: none -> 240 us  [run_block(): pl.pallas_call(block_kernel, out_shape=(jax.ShapeDtypeStruct(tok.shape, b...]
    all_gather x6 -> x0, waiting for transfers between devices: 219 us -> none  [the longest x1 47.8 us: local(): lax.all_gather(h_two_f.astype(jnp.bfloat16), 'tensor', axis=0, tiled=True)]
    dot_general x26 -> x0, matrix products: 91.1 us -> none  [the longest x1 15.5 us: local(): jnp.dot(h_two, ffn_half[0], preferred_element_type=jnp.float32) * scale_d]
    psum x1 -> x0, blocking collectives: 39.9 us -> none  [local(): lax.psum(jnp.stack([d_gain_one, d_bias_one, d_gain_two, d_bias_two]), ('d...]
    reduce_sum x12 -> x0, other arithmetic: 30.6 us -> none  [the longest x2 10.3 us: layer_norm(): row_mean = jnp.mean(inputs, axis=-1, keepdims=True)]
    unnamed x91 -> x38, local copies, waits for them, and re-layouts: 30.6 us -> 4.17 us
    mul x4 -> x0, local copies, waits for them, and re-layouts: 9.63 us -> none  [the longest x1 5.44 us: local(): dot_last(d_hidden, ffn_half[0]) * scale_d]
  transfers between devices with their start and end apart: 12 -> 0, of which waited for: 12 -> 0; matrix products, arithmetic and copies ran while one was open for 15% -> 0% of each run, Pallas kernels for 0% -> 0%
where the time goes in v1:
time: 263 us; the launch traced here: 261 us
  Pallas kernels  240 us (91%)
  other arithmetic  15.2 us (6%)
  local copies, waits for them, and re-layouts  4.67 us (2%)
    pallas_call x1, Pallas kernels, run_block(): pl.pallas_call(block_kernel, out_shape=(jax.ShapeDtypeStruct(tok.shape, b...  240 us
    add x3, other arithmetic, adam_update(): new_ema = ema_value * ema_weight + (1.0 - ema_value) * new_weight  5.68 us

profile of v1, /device:TPU:5, one launch (start us, length us, event | category | flops | bytes accessed | tf_op | source)
XLA Modules:
  0.0 260.9 jit_solution(2824735953790503690)
XLA Ops:
  0.6 0.0 copy-start.15
  0.7 0.0 copy-start.16
  0.7 0.0 copy-start.17
  0.7 2.1 convert_element_type.31.ffn_in
  2.8 1.8 convert_element_type.30.attn_in
  4.6 0.0 copy-done.15
  4.6 0.0 copy-done.16
  4.6 0.3 scatter.11
  4.8 0.0 copy-done.17
  4.9 0.2 scatter.14.info_in
  5.1 0.0 copy-start.12
  5.1 0.6 copy-done.12
  5.7 0.0 copy-start.10
  5.7 0.0 copy-start.13
  5.7 0.0 copy-start.14
  5.7 240.2 %block.1 = (bf16[256,1024]{1,0:T(8,128)(2,1)}, bf16[256,1024]{1,0:T(8,128)(2,1)}, bf16[2,4,128,256]{3,2,1,0:T(8,128)(2,1)}, bf16[2,2,128,1024]{3,2,1,0:T(8,128)(2,1)}, f32[8,1024]{1,0:T(8,128)}) custom-call(bf16[256,1024]{1,0:T(8,128)(2,1)} %tok_in.1, bf16[256,1024]{1,0:T(8,128)(2,1)} %cot_in.1, s32[8,1024]{1,0:T(8,128)} %copy-done.12, ...), custom_call_target="tpu_custom_call" | custom-call | flops 30000001024 | bytes 30000000 | tf_op jit(solution)/shard_map/block/pallas_call | solution.py:1038
  246.0 0.0 copy-done.10
  246.0 0.0 copy-done.13
  246.0 0.0 copy-done.14
  246.0 1.4 multiply_add_fusion.6
  247.4 0.0 copy-start.11
  247.4 0.6 pad_maximum_fusion.2
  248.0 2.2 multiply_add_fusion.2
  250.3 0.0 copy-done.11
  250.3 0.0 copy-start.1
  250.3 0.0 copy-start.4
  250.3 0.0 copy-start.6
  250.3 1.5 pad_maximum_fusion
  251.8 0.1 copy-done.1
  251.9 0.5 copy-done.4
  252.4 0.0 copy-start
  252.4 0.0 copy-start.2
  252.4 0.0 copy-start.3
  252.4 0.2 multiply_add_fusion.5
  252.6 1.1 pad_maximum_fusion.1
  253.7 0.0 copy-done.6
  253.7 0.8 copy-done
  254.4 0.3 copy-done.2
  254.7 0.3 copy-done.3
  255.0 0.0 copy-start.5
  255.0 0.0 copy-start.9
  255.0 2.7 %multiply_add_fusion = (f32[2,128,1024]{2,1,0:T(8,128)}, f32[2,128,1024]{2,1,0:T(8,128)}, f32[2,128,1024]{2,1,0:T(8,128)}) fusion(f32[2,128,1024]{2,1,0:T(8,128)S(1)} %copy-done.6, f32[2,128,1024]{2,1,0:T(8,128)S(1)} %copy-done.3, f32[2,2,128,1024]{3,2,1,0:T(8,128)S(1)} %copy-done, bf16[2,2,128,1024]{3,2,1,0:T(8,128)(2,1)S(1)} %copy-done.2), kind=kLoop, calls=%fused_computation.12 | loop fusion | flops 5767168 | bytes 8388608 | tf_op jit(solution)/shard_map/add | solution.py:51
  257.7 0.0 copy-done.5
  257.7 0.0 copy-done.9
  257.7 0.0 copy-start.8
  257.7 0.0 copy-start.7
  257.7 1.6 multiply_add_fusion.3
  259.3 0.0 copy-done.8
  259.3 0.8 copy.33
  260.1 0.0 copy-done.7
  260.1 0.8 copy.34
  (2 shorter events, 0.0 us)
Async XLA Ops:
  0.6 3.9 %copy-start.15 = (s32[1,1024]{1,0:T(1,128)S(1)}, s32[1,1024]{1,0:T(1,128)}, u32[]{:S(2)}) copy-start(s32[1,1024]{1,0:T(1,128)} %param.24) | copy-start | bytes 12292
  0.7 3.9 %copy-start.16 = (s32[1,256]{1,0:T(1,128)S(1)}, s32[1,256]{1,0:T(1,128)}, u32[]{:S(2)}) copy-start(s32[1,256]{1,0:T(1,128)} %param.23) | copy-start | bytes 3076
  0.7 4.2 %copy-start.17 = (s32[1,4]{1,0:T(1,128)S(1)}, s32[1,4]{1,0:T(1,128)}, u32[]{:S(2)}) copy-start(s32[1,4]{1,0:T(1,128)} %param.25) | copy-start | bytes 52
  5.1 0.6 copy-start.12
  5.7 240.2 %copy-start.10 = (f32[2,4,1024]{2,1,0:T(4,128)S(1)}, f32[2,4,1024]{2,1,0:T(4,128)}, u32[]{:S(2)}) copy-start(f32[2,4,1024]{2,1,0:T(4,128)} %param.33) | copy-start | bytes 98308
  5.7 240.2 %copy-start.13 = (f32[4,1024]{1,0:T(4,128)S(1)}, f32[4,1024]{1,0:T(4,128)}, u32[]{:S(2)}) copy-start(f32[4,1024]{1,0:T(4,128)} %norm_in.1) | copy-start | bytes 49156
  5.7 240.3 %copy-start.14 = (f32[4,1024]{1,0:T(4,128)S(1)}, f32[4,1024]{1,0:T(4,128)}, u32[]{:S(2)}) copy-start(f32[4,1024]{1,0:T(4,128)} %param.34) | copy-start | bytes 49156
  247.4 2.9 %copy-start.11 = (f32[4,1024]{1,0:T(4,128)}, f32[4,1024]{1,0:T(4,128)S(1)}, u32[]{:S(2)}) copy-start(f32[4,1024]{1,0:T(4,128)S(1)} %get-tuple-element.93) | copy-start | bytes 49156
  250.3 1.6 copy-start.1
  250.3 2.1 copy-start.4
  250.3 3.3 %copy-start.6 = (f32[2,128,1024]{2,1,0:T(8,128)S(1)}, f32[2,128,1024]{2,1,0:T(8,128)}, u32[]{:S(2)}) copy-start(f32[2,128,1024]{2,1,0:T(8,128)} %param.31) | copy-start | bytes 3145732
  252.4 2.0 copy-start
  252.4 2.3 copy-start.2
  252.4 2.6 %copy-start.3 = (f32[2,128,1024]{2,1,0:T(8,128)S(1)}, f32[2,128,1024]{2,1,0:T(8,128)}, u32[]{:S(2)}) copy-start(f32[2,128,1024]{2,1,0:T(8,128)} %param.29) | copy-start | bytes 3145732
  255.0 2.7 %copy-start.5 = (f32[4,128,256]{2,1,0:T(8,128)S(1)}, f32[4,128,256]{2,1,0:T(8,128)}, u32[]{:S(2)}) copy-start(f32[4,128,256]{2,1,0:T(8,128)} %param.26) | copy-start | bytes 1572868
  255.0 2.7 %copy-start.9 = (f32[4,128,256]{2,1,0:T(8,128)S(1)}, f32[4,128,256]{2,1,0:T(8,128)}, u32[]{:S(2)}) copy-start(f32[4,128,256]{2,1,0:T(8,128)} %param.28) | copy-start | bytes 1572868
  257.7 1.6 copy-start.8
  257.7 2.4 copy-start.7

commit v2 on v1

--- a/solution.py
+++ b/solution.py
@@ -257,6 +257,7 @@
 
 MESH = pl.DeviceIdType.MESH
 TOK = 256
+WIDE = 512
 CHUNK = 32
 PIECES = ("qkv", "out", "up", "down")
 
@@ -309,7 +310,9 @@
 def block_kernel(
     tok_in,
     cot_in,
-    info_in,
+    pos_in,
+    seg_in,
+    flag_in,
     attn_in,
     ffn_in,
     norm_in,
@@ -350,7 +353,7 @@
     dk_tmp,
     dv_tmp,
     ffn_sum,
-    attn_stage,
+    stage,
     attn_sum,
     ffn_box,
     attn_box,
@@ -372,6 +375,9 @@
     grad_own_recv,
     norm_send_sem,
     norm_recv_sem,
+    attn_half,
+    load_sem,
+    info_in,
 ):
     width = freq_in.shape[1]
     scale_d = width ** (-0.5)
@@ -406,6 +412,20 @@
             src_ref=src, dst_ref=dst, send_sem=send, recv_sem=recv, device_id=device, device_id_type=MESH
         )
 
+    def load_copy(i):
+        if i < 4:
+            src, dst = attn_in.at[i], acc_a.at[0:128, pl.ds(i * 256, 256)]
+        else:
+            src, dst = ffn_in.at[i - 4], acc_b.at[pl.ds((i - 4) * 128, 128), :]
+        return pltpu.make_async_copy(src, dst, load_sem.at[i])
+
+    for i in range(6):
+        load_copy(i).start()
+    info_in[...] = jnp.zeros_like(info_in)
+    info_in[0:1, :] = seg_in[...]
+    info_in[1:2, 0:TOK] = pos_in[...]
+    info_in[2:3, 0 : flag_in.shape[1]] = flag_in[...]
+
     barrier = pltpu.get_barrier_semaphore()
     peers = list(nears)
     for dd in (d, d_sib):
@@ -414,6 +434,9 @@
     peers = peers[:3] + peers[4:]
     for peer in peers:
         pl.semaphore_signal(barrier, inc=1, device_id=peer, device_id_type=MESH)
+    for i in range(4):
+        load_copy(i).wait()
+        attn_half[i] = acc_a[0:128, i * 256 : (i + 1) * 256].astype(jnp.bfloat16)
     pl.semaphore_wait(barrier, len(peers))
 
     own = aligned(par * TOK, TOK)
@@ -445,10 +468,10 @@
 
     def piece_source(piece):
         if piece == 0:
-            return attn_in.at[0:3]
+            return attn_half.at[0:3]
         if piece == 1:
-            return attn_in.at[3]
-        return ffn_in.at[piece - 2]
+            return attn_half.at[3]
+        return send_b.at[pl.ds((piece - 2) * 128, 128), :]
 
     def one_copy(piece, k):
         dst = piece_view(piece, par, aligned(d * 128, 128))
@@ -482,8 +505,14 @@
                 one_copy(piece, k).wait_send()
 
     def two_copy(piece, k):
-        view = piece_view(piece, core, aligned(col * 256, 256))
-        return remote(view, view, two_send.at[piece, k], two_recv.at[piece, k], nears[k])
+        if k < 2:
+            rows, target = aligned(col * 256, 256), nears[k]
+        elif k == 2:
+            rows, target = aligned(near_cols[0] * 256, 128), nears[1]
+        else:
+            rows, target = aligned(near_cols[1] * 256 + 128, 128), nears[0]
+        view = piece_view(piece, core, rows)
+        return remote(view, view, two_send.at[piece, k], two_recv.at[piece, k], target)
 
     def sib_copy(piece, k):
         which = col if k == 0 else near_cols[k - 1]
@@ -496,28 +525,43 @@
             pltpu.make_async_copy(
                 piece_source(piece), piece_view(piece, core, rows), one_recv.at[piece, c0]
             ).wait()
-        for k in range(3):
+        for k in range(2):
             two_copy(piece, k).start()
         sib_copy(piece, 0).start()
 
     def relay(piece):
-        for k in range(3):
+        for k in range(2):
             two_copy(piece, k).wait_recv()
+            two_copy(piece, k + 2).start()
             sib_copy(piece, k + 1).start()
+
+    def relay_last(piece):
+        for k in range(2, 4):
+            two_copy(piece, k).wait_recv()
+        sib_copy(piece, 3).start()
 
     def ready(piece):
         for k in range(4):
             sib_copy(piece, k).wait_recv()
 
     def sent(piece):
-        for k in range(3):
+        for k in range(4):
             two_copy(piece, k).wait_send()
-        for k in range(4):
             sib_copy(piece, k).wait_send()
 
     swap_in(info_in, info, 0)
     one_start(0)
     swap_in(tok_in, tok_buf, 1)
+    one_start(1)
+    for i in range(2):
+        load_copy(4 + i).wait()
+
+        def round_rows(step, carry):
+            rows = aligned(i * 128 + step * CHUNK, CHUNK)
+            send_b[rows, :] = acc_b[rows, :].astype(jnp.bfloat16)
+            return carry
+
+        lax.fori_loop(0, 128 // CHUNK, round_rows, 0)
     swap_wait(info_in, info, 0)
 
     seg_first = (2 * core + par) * TOK
@@ -543,13 +587,6 @@
         return carry
 
     lax.fori_loop(0, TOK // CHUNK, encode, 0)
-
-    spread(0)
-    one_start(1)
-    swap_in(cot_in, g_all.at[own, :], 2)
-    one_start(2)
-    one_start(3)
-    swap_wait(tok_in, tok_buf, 1)
 
     def norm_first(step, carry):
         rows = aligned(step * CHUNK, CHUNK)
@@ -560,18 +597,28 @@
         h_one[row, :] = (unit * norm_in[0:1, :] + norm_in[1:2, :]).astype(jnp.bfloat16)
         return carry
 
-    lax.fori_loop(0, TOK // CHUNK, norm_first, 0)
-
     def pair_copy(buf, index):
         return remote(buf.at[own, :], buf.at[own, :], act_send.at[index], act_recv.at[index], pair)
 
-    pair_copy(h_one, 3).start()
+    def embed_cells():
+        swap_wait(tok_in, tok_buf, 1)
+        lax.fori_loop(0, TOK // CHUNK, norm_first, 0)
+        pair_copy(h_one, 3).start()
+
+    @pl.when(home)
+    def _():
+        swap_in(cot_in, g_all.at[own, :], 2)
+        embed_cells()
+        swap_wait(cot_in, g_all.at[own, :], 2)
+        pair_copy(g_all, 4).start()
+
+    spread(0)
     relay(0)
+    relay_last(0)
     spread(1)
+    pl.when(jnp.logical_not(home))(embed_cells)
+    one_start(2)
     ready(0)
-    swap_wait(cot_in, g_all.at[own, :], 2)
-    pair_copy(g_all, 4).start()
-    spread(2)
 
     def project(first):
         rows = aligned(first * TOK, TOK)
@@ -592,21 +639,22 @@
 
     project(par)
     kv_copy(par, 5).start()
+    relay(1)
     pair_copy(h_one, 3).wait_recv()
+    one_start(3)
     project(flip(par))
     kv_copy(flip(par), 6).start()
-    relay(1)
-    spread(3)
+    relay_last(1)
     kv_copy(par, 5).wait_recv()
     kv_copy(flip(par), 6).wait_recv()
+    spread(2)
 
     lane_half = lax.broadcasted_iota(jnp.int32, (TOK, 128), 1)
     lane_masks = (lane_half < HD, lane_half >= HD)
 
-    def attend(i, carry):
-        jj = lax.div(i, 2)
-        rows = aligned(lax.rem(i, 2) * TOK, TOK)
-        q_rows = aligned(core * 512 + lax.rem(i, 2) * TOK, TOK)
+    def attend(first, jj):
+        rows = aligned(first * TOK, TOK)
+        q_rows = aligned(core * 512 + first * TOK, TOK)
         h = lax.div(jj, 2)
         lanes = aligned(lax.rem(jj, 2) * 128, 128)
         queries = qkv[0, h, q_rows, lanes] * jnp.bfloat16(score_scale)
@@ -624,39 +672,56 @@
             prob[2 * jj + a, rows, :] = share
             outs.append(contract(share, vals, 1, 0))
         att[h, rows, lanes] = jnp.where(lane_masks[0], outs[0], outs[1]).astype(jnp.bfloat16)
-        return carry
-
-    lax.fori_loop(0, 8, attend, 0)
+
+    def attend_rows(first):
+        def step(jj, carry):
+            attend(first, jj)
+            return carry
+
+        lax.fori_loop(0, 4, step, 0)
+
+    attend_rows(flip(par))
+
+    @pl.when(jnp.logical_not(home))
+    def _():
+        swap_in(cot_in, g_all.at[own, :], 2)
 
     ready(1)
-    relay(2)
-
-    def split_product(product, scale, send_buf, recv_buf, acc, index, steps):
-        def step_send(n, carry):
-            lanes = aligned(n * TOK, TOK)
+
+    def product_fill(product, scale, send_buf):
+        def step(n, carry):
+            lanes = aligned(n * WIDE, WIDE)
             send_buf[:, lanes] = (product(other, n) * scale).astype(jnp.bfloat16)
             return carry
 
-        lax.fori_loop(0, steps, step_send, 0)
+        lax.fori_loop(0, width // WIDE, step, 0)
+
+    def product_send(product, scale, send_buf, recv_buf, index):
+        product_fill(product, scale, send_buf)
         remote(send_buf, recv_buf, act_send.at[index], act_recv.at[index], pair).start()
 
-        def step_keep(n, carry):
-            lanes = aligned(n * TOK, TOK)
+    def product_keep(product, scale, acc):
+        def step(n, carry):
+            lanes = aligned(n * WIDE, WIDE)
             acc[:, lanes] = product(own, n) * scale
             return carry
 
-        lax.fori_loop(0, steps, step_keep, 0)
+        lax.fori_loop(0, width // WIDE, step, 0)
 
     def split_wait(send_buf, recv_buf, index):
         remote(send_buf, recv_buf, act_send.at[index], act_recv.at[index], pair).wait()
 
     def out_product(rows, n):
-        outs = aligned(n * TOK, TOK)
+        outs = aligned(n * WIDE, WIDE)
         total = contract(att[0, rows, :], attn_w[0, 3, outs, :], 1, 1)
         return total + contract(att[1, rows, :], attn_w[1, 3, outs, :], 1, 1)
 
-    split_product(out_product, out_scale, send_a, recv_a, acc_a, 7, 4)
-    relay(3)
+    product_send(out_product, out_scale, send_a, recv_a, 7)
+    relay(2)
+    attend_rows(par)
+    relay_last(2)
+    spread(3)
+    product_keep(out_product, out_scale, acc_a)
     split_wait(send_a, recv_a, 7)
 
     def norm_second(step, carry):
@@ -670,46 +735,51 @@
 
     lax.fori_loop(0, TOK // CHUNK, norm_second, 0)
     pair_copy(h_two, 8).start()
-    pair_copy(g_all, 4).wait_recv()
+
+    @pl.when(jnp.logical_not(home))
+    def _():
+        swap_wait(cot_in, g_all.at[own, :], 2)
+        pair_copy(g_all, 4).start()
+
     ready(2)
-    ready(3)
-
-    def feed(first):
+
+    def feed_up(first):
         rows = aligned(first * TOK, TOK)
 
         def step(i, carry):
-            h = lax.div(i, 4)
-            lanes = aligned(lax.rem(i, 4) * 256, 256)
+            h = lax.div(i, 2)
+            lanes = aligned(lax.rem(i, 2) * 512, 512)
             hidden = contract(h_two[rows, :], ffn_w[h, 0, :, lanes], 1, 0) * scale_d
-            d_act = contract(g_all[rows, :], ffn_w[h, 1, :, lanes], 1, 0) * scale_f
             gate = 0.5 + 0.5 * lax.erf(hidden * np.float32(np.sqrt(0.5)))
             act[h, rows, lanes] = (hidden * gate).astype(jnp.bfloat16)
             bell = jnp.exp(-0.5 * hidden * hidden) * np.float32(1.0 / np.sqrt(2.0 * np.pi))
-            d_hid[h, rows, lanes] = (d_act * (gate + hidden * bell)).astype(jnp.bfloat16)
+            d_hid[h, rows, lanes] = (gate + hidden * bell).astype(jnp.bfloat16)
             return carry
 
-        lax.fori_loop(0, 8, step, 0)
-
-    feed(par)
-    pair_copy(h_two, 8).wait_recv()
-    feed(flip(par))
+        lax.fori_loop(0, 4, step, 0)
+
+    def feed_back(first):
+        rows = aligned(first * TOK, TOK)
+
+        def step(i, carry):
+            h = lax.div(i, 2)
+            lanes = aligned(lax.rem(i, 2) * 512, 512)
+            d_act = contract(g_all[rows, :], ffn_w[h, 1, :, lanes], 1, 0) * scale_f
+            slope = d_hid[h, rows, lanes].astype(jnp.float32)
+            d_hid[h, rows, lanes] = (d_act * slope).astype(jnp.bfloat16)
+            return carry
+
+        lax.fori_loop(0, 4, step, 0)
 
     def hid_product(rows, n):
-        outs = aligned(n * TOK, TOK)
+        outs = aligned(n * WIDE, WIDE)
         total = contract(d_hid[0, rows, :], ffn_w[0, 0, outs, :], 1, 1)
         return total + contract(d_hid[1, rows, :], ffn_w[1, 0, outs, :], 1, 1)
 
-    split_product(hid_product, scale_d, send_a, recv_a, acc_a, 9, 4)
-
     def down_product(rows, n):
-        outs = aligned(n * TOK, TOK)
+        outs = aligned(n * WIDE, WIDE)
         total = contract(act[0, rows, :], ffn_w[0, 1, outs, :], 1, 1)
         return total + contract(act[1, rows, :], ffn_w[1, 1, outs, :], 1, 1)
-
-    split_product(down_product, scale_f, send_b, recv_b, acc_b, 10, 4)
-    for piece in range(4):
-        one_sent(piece)
-        sent(piece)
 
     def grad_tile(kind, m, h, tile):
         cells = aligned(tile * 256, 256)
@@ -722,7 +792,7 @@
         return contract(left, right, 0, 0) * (scale_d if m == 0 else scale_f)
 
     def stage_view(kind, m, rows):
-        return attn_stage.at[m, rows, :] if kind == 0 else ffn_w.at[0, m, rows, :]
+        return stage.at[rows, pl.ds(m * 256, 256)] if kind == 0 else stage.at[rows, :]
 
     def sum_view(kind, m, rows):
         return attn_sum.at[m, rows, :] if kind == 0 else ffn_sum.at[m, rows, :]
@@ -744,8 +814,8 @@
     def grads_sibling(kind, m):
         def step(tile, carry):
             rows = aligned(tile * 256, 256)
-            stage = stage_view(kind, m, rows)
-            stage[...] = grad_tile(kind, m, flip(core), tile).astype(jnp.bfloat16)
+            view = stage_view(kind, m, rows)
+            view[...] = grad_tile(kind, m, flip(core), tile).astype(jnp.bfloat16)
             tile_copy(kind, m, tile).start()
             return carry
 
@@ -758,35 +828,62 @@
         y_new = y_bit + to_y - 2 * y_bit * to_y
         return 2 * y_new + x_new
 
+    def box_rows(k):
+        place = (near_cols[2], near_cols[2], near_cols[0], near_cols[1], near_cols[0], near_cols[1])[k]
+        return aligned(place * 256 + (0, 1, 0, 1, 1, 0)[k] * 128, 128)
+
     def box_view(kind, m, k):
         return attn_box.at[k, m] if kind == 0 else ffn_box.at[k, m]
 
     def box_copy(kind, m, k):
-        place = tile_place(k)
         index = slot(kind, m)
         return remote(
-            sum_view(kind, m, aligned(place * 256, 256)),
+            sum_view(kind, m, box_rows(k)),
             box_view(kind, m, k),
             grad_box_send.at[index, k],
             grad_box_recv.at[index, k],
-            (2 * place + core, t),
+            nears[k % 2],
         )
 
+    def stage_sent(kind, m):
+        for tile in range(4):
+            tile_copy(kind, m, tile).wait_send()
+
     def grads_own(kind, m):
-        def step(k, carry):
+        def tile(k):
             place = tile_place(k)
             total = grad_tile(kind, m, core, place)
             tile_copy(kind, m, place).wait_recv()
             view = sum_view(kind, m, aligned(place * 256, 256))
             view[...] = (total + view[...].astype(jnp.float32)).astype(jnp.bfloat16)
 
-            @pl.when(k < 3)
+        def step(k, carry):
+            tile(k)
+
+            @pl.when(k == 0)
             def _():
-                box_copy(kind, m, k).start()
+                box_copy(kind, m, 0).start()
+                box_copy(kind, m, 1).start()
+
+            @pl.when(k == 1)
+            def _():
+                box_copy(kind, m, 2).start()
+
+            @pl.when(k == 2)
+            def _():
+                box_copy(kind, m, 3).start()
 
             return carry
 
         lax.fori_loop(0, 4, step, 0)
+
+    def grads_mid(kind, m):
+        for k, came in ((4, 1), (5, 0)):
+            box_copy(kind, m, came).wait_recv()
+            view = sum_view(kind, m, box_rows(k))
+            box = box_view(kind, m, came)
+            view[...] = (view[...].astype(jnp.float32) + box[...].astype(jnp.float32)).astype(jnp.bfloat16)
+            box_copy(kind, m, k).start()
 
     def own_copy(kind, m, c0):
         rows = aligned(col * 256 + c0 * 128, 128)
@@ -804,20 +901,14 @@
         return jnp.logical_and(core == c0, t == quarter)
 
     def grads_columns(kind, m):
-        for k in range(3):
-            box_copy(kind, m, k).wait_recv()
-
-        def step(i, carry):
-            rows = aligned(col * 256 + i * CHUNK, CHUNK)
-            part = aligned(i * CHUNK, CHUNK)
-            view = sum_view(kind, m, rows)
+        for c0, came in ((0, (2, 5)), (1, (3, 4))):
+            for k in came:
+                box_copy(kind, m, k).wait_recv()
+            view = sum_view(kind, m, aligned(col * 256 + c0 * 128, 128))
             total = view[...].astype(jnp.float32)
-            for k in range(3):
-                total = total + box_view(kind, m, k)[part, :].astype(jnp.float32)
+            for k in came:
+                total = total + box_view(kind, m, k)[...].astype(jnp.float32)
             view[...] = total.astype(jnp.bfloat16)
-            return carry
-
-        lax.fori_loop(0, 256 // CHUNK, step, 0)
         for c0 in range(2):
 
             @pl.when(own_is_here(c0))
@@ -838,9 +929,7 @@
             src = sum_view(kind, m, aligned(col * 256, 128))
             dst = attn_parts.at[k, m] if kind == 0 else ffn_parts.at[k, m]
             pltpu.make_async_copy(src, dst, grad_own_recv.at[index, k]).wait()
-        for k in range(4):
-            tile_copy(kind, m, k).wait_send()
-        for k in range(3):
+        for k in range(6):
             box_copy(kind, m, k).wait_send()
         for c0 in range(2):
 
@@ -848,8 +937,27 @@
             def _():
                 own_copy(kind, m, c0).wait_send()
 
+    feed_up(par)
+    relay(3)
+    pair_copy(h_two, 8).wait_recv()
+    feed_up(flip(par))
+    relay_last(3)
+    pair_copy(g_all, 4).wait_recv()
+    grads_sibling(1, 1)
+    ready(3)
+    feed_back(flip(par))
+    product_send(hid_product, scale_d, send_a, recv_a, 9)
+    feed_back(par)
+    grads_own(1, 1)
+    stage_sent(1, 1)
     grads_sibling(1, 0)
-    grads_sibling(1, 1)
+    product_keep(hid_product, scale_d, acc_a)
+    grads_mid(1, 1)
+    grads_own(1, 0)
+    for piece in range(4):
+        one_sent(piece)
+        sent(piece)
+    product_fill(down_product, scale_f, send_b)
 
     split_wait(send_a, recv_a, 9)
 
@@ -879,20 +987,7 @@
     norm_acc[...] = jnp.zeros_like(norm_acc)
     lax.fori_loop(0, TOK // CHUNK, back_second, 0)
     pair_copy(d_mid_all, 11).start()
-
-    grads_own(1, 0)
-    grads_own(1, 1)
-
-    split_wait(send_b, recv_b, 10)
-
-    def finish_out(step, carry):
-        rows = aligned(step * CHUNK, CHUNK)
-        total = x_mid[rows, :] + (acc_b[rows, :] + recv_b[rows, :].astype(jnp.float32))
-        tok_buf[rows, :] = total.astype(jnp.bfloat16)
-        return carry
-
-    lax.fori_loop(0, TOK // CHUNK, finish_out, 0)
-    swap_in(tok_buf, tok_out, 12)
+    product_keep(down_product, scale_f, acc_b)
 
     def back_out(first):
         rows = aligned(first * TOK, TOK)
@@ -904,41 +999,40 @@
 
         lax.fori_loop(0, 2, step, 0)
 
-    back_out(par)
-    pair_copy(d_mid_all, 11).wait_recv()
-    back_out(flip(par))
-    grads_sibling(0, 3)
-
-    def attend_back(jj, carry):
+    def attend_back(first, last, jj):
         h = lax.div(jj, 2)
         lanes = aligned(lax.rem(jj, 2) * 128, 128)
+        kept = aligned(jj * 128, 128)
         keys = qkv[1, h, :, lanes]
         vals = qkv[2, h, :, lanes]
+        rows = aligned(first * TOK, TOK)
+        q_rows = aligned(core * 512 + first * TOK, TOK)
+        queries = qkv[0, h, q_rows, lanes] * jnp.bfloat16(score_scale)
+        d_outs = d_att[h, rows, lanes]
+        inner = d_outs.astype(jnp.float32) * att[h, rows, lanes].astype(jnp.float32)
+        dqs = []
         dk_total = None
         dv_total = None
-        for part in range(2):
-            rows = pl.ds(part * TOK, TOK)
-            q_rows = aligned(core * 512 + part * TOK, TOK)
-            queries = qkv[0, h, q_rows, lanes] * jnp.bfloat16(score_scale)
-            d_outs = d_att[h, rows, lanes]
-            inner = d_outs.astype(jnp.float32) * att[h, rows, lanes].astype(jnp.float32)
-            dqs = []
-            for a in range(2):
-                share = prob[2 * jj + a, rows, :]
-                d_out = jnp.where(lane_masks[a], d_outs, jnp.bfloat16(0))
-                query = jnp.where(lane_masks[a], queries, jnp.bfloat16(0))
-                row_sum = jnp.sum(jnp.where(lane_masks[a], inner, 0.0), axis=1, keepdims=True)
-                d_prob = contract(d_out, vals, 1, 1)
-                d_score = (share.astype(jnp.float32) * (d_prob - row_sum)).astype(jnp.bfloat16)
-                dqs.append(contract(d_score, keys, 1, 0))
-                dk = contract(query, d_score, 0, 0)
-                dv = contract(d_out, share, 0, 0)
-                dk_total = dk if dk_total is None else dk_total + dk
-                dv_total = dv if dv_total is None else dv_total + dv
-            d_query = jnp.where(lane_masks[0], dqs[0], dqs[1]) * score_scale
-            d_qkv[0, h, rows, lanes] = d_query.astype(jnp.bfloat16)
-        dk_tmp[...] = dk_total
-        dv_tmp[...] = dv_total
+        for a in range(2):
+            share = prob[2 * jj + a, rows, :]
+            d_out = jnp.where(lane_masks[a], d_outs, jnp.bfloat16(0))
+            query = jnp.where(lane_masks[a], queries, jnp.bfloat16(0))
+            row_sum = jnp.sum(jnp.where(lane_masks[a], inner, 0.0), axis=1, keepdims=True)
+            d_prob = contract(d_out, vals, 1, 1)
+            d_score = (share.astype(jnp.float32) * (d_prob - row_sum)).astype(jnp.bfloat16)
+            dqs.append(contract(d_score, keys, 1, 0))
+            dk = contract(query, d_score, 0, 0)
+            dv = contract(d_out, share, 0, 0)
+            dk_total = dk if dk_total is None else dk_total + dk
+            dv_total = dv if dv_total is None else dv_total + dv
+        d_query = jnp.where(lane_masks[0], dqs[0], dqs[1]) * score_scale
+        d_qkv[0, h, rows, lanes] = d_query.astype(jnp.bfloat16)
+        if not last:
+            ffn_w[1, 0, kept, :] = dk_total.astype(jnp.bfloat16)
+            ffn_w[1, 1, kept, :] = dv_total.astype(jnp.bfloat16)
+            return
+        dk_tmp[...] = dk_total + ffn_w[1, 0, kept, :].astype(jnp.float32)
+        dv_tmp[...] = dv_total + ffn_w[1, 1, kept, :].astype(jnp.float32)
         mine = aligned(core * 512, 512)
         theirs = aligned(flip(core) * 512, 512)
         d_qkv[1, h, :, lanes] = jnp.transpose(dk_tmp[:, mine]).astype(jnp.bfloat16)
@@ -946,12 +1040,28 @@
         kv_send[jj, 0] = jnp.transpose(dk_tmp[:, theirs]).astype(jnp.bfloat16)
         kv_send[jj, 1] = jnp.transpose(dv_tmp[:, theirs]).astype(jnp.bfloat16)
         kv_grad_copy(jj).start()
-        return carry
+
+    def attend_back_rows(first, last):
+        def step(jj, carry):
+            attend_back(first, last, jj)
+            return carry
+
+        lax.fori_loop(0, 4, step, 0)
 
     def kv_grad_copy(jj):
         return remote(kv_send.at[jj], kv_recv.at[jj], act_send.at[13 + jj], act_recv.at[13 + jj], sib)
 
-    lax.fori_loop(0, 4, attend_back, 0)
+    back_out(par)
+    grads_columns(1, 1)
+    grads_mid(1, 0)
+    attend_back_rows(par, False)
+    pair_copy(d_mid_all, 11).wait_recv()
+    remote(send_b, recv_b, act_send.at[10], act_recv.at[10], pair).start()
+    back_out(flip(par))
+    attend_back_rows(flip(par), True)
+    grads_columns(1, 0)
+    stage_sent(1, 0)
+    grads_sibling(0, 3)
 
     def join_kv(jj, carry):
         kv_grad_copy(jj).wait()
@@ -962,12 +1072,10 @@
             d_qkv[m + 1, h, :, lanes] = total.astype(jnp.bfloat16)
         return carry
 
-    grads_columns(1, 0)
-    grads_columns(1, 1)
     lax.fori_loop(0, 4, join_kv, 0)
 
     def first_product(rows, n):
-        outs = aligned(n * TOK, TOK)
+        outs = slice(None) if n is None else aligned(n * WIDE, WIDE)
         total = None
         for h in range(2):
             for m in range(3):
@@ -975,20 +1083,41 @@
                 total = part if total is None else total + part
         return total
 
-    split_product(first_product, scale_d, send_a, recv_a, acc_a, 17, 4)
+    def first_copy(i):
+        rows = pl.ds(i * 128, 128)
+        return remote(
+            send_a.at[rows, :], recv_a.at[rows, :], act_send.at[19 + i], act_recv.at[19 + i], pair
+        )
+
+    for i in range(2):
+        part = first_product(aligned(flip(par) * TOK + i * 128, 128), None) * scale_d
+        send_a[i * 128 : (i + 1) * 128, :] = part.astype(jnp.bfloat16)
+        first_copy(i).start()
+
     for m in range(3):
         grads_sibling(0, m)
+    product_keep(first_product, scale_d, acc_a)
     grads_own(0, 3)
     for m in range(3):
         grads_own(0, m)
 
-    split_wait(send_a, recv_a, 17)
-    swap_sent(tok_buf, tok_out, 12)
-    swap_wait(tok_buf, tok_out, 12)
-
+    split_wait(send_b, recv_b, 10)
+
+    def finish_out(step, carry):
+        rows = aligned(step * CHUNK, CHUNK)
+        total = x_mid[rows, :] + (acc_b[rows, :] + recv_b[rows, :].astype(jnp.float32))
+        tok_buf[rows, :] = total.astype(jnp.bfloat16)
+        return carry
+
+    lax.fori_loop(0, TOK // CHUNK, finish_out, 0)
+    swap_in(tok_buf, tok_out, 12)
+
+
+    for m in (3, 0, 1):
+        grads_mid(0, m)
     def back_first(step, carry):
         def out(rows, result):
-            tok_buf[rows, :] = result.astype(jnp.bfloat16)
+            send_b[rows, :] = result.astype(jnp.bfloat16)
 
         add = d_mid[aligned(step * CHUNK, CHUNK), :]
         d_gain, d_bias = back_norm(step, x_embed, norm_in[0:1, :], add, acc_a, out)
@@ -996,26 +1125,75 @@
         norm_acc[1] = norm_acc[1] + d_bias
         return carry
 
-    lax.fori_loop(0, TOK // CHUNK, back_first, 0)
-    swap_in(tok_buf, grad_out, 18)
+    def grad_copy(i):
+        rows = pl.ds(i * 128, 128)
+        return send_b.at[rows, :], grad_out.at[rows, :], 17 + i
+
+    for i in range(2):
+        first_copy(i).wait()
+        lax.fori_loop(4 * i, 4 * i + 4, back_first, 0)
+        swap_in(*grad_copy(i))
 
     for row in range(4):
         norm_out[row : row + 1, :] = jnp.sum(norm_acc[row], axis=0, keepdims=True)
     norm_out[4:8, :] = jnp.zeros((4, width), jnp.float32)
-    for i, peer in enumerate((sib, nears[0], nears[1], pair, (d, t_far))):
-        copy = remote(norm_out, norm_recv.at[i], norm_send_sem.at[i], norm_recv_sem.at[i], peer)
-        copy.start()
-        copy.wait()
-        norm_out[...] = norm_out[...] + norm_recv[i]
-
-    for m in (3, 0, 1, 2):
+    mine = 4 * core + t
+    norm_recv[mine] = norm_out[...]
+
+    def norm_copy(i):
+        return remote(
+            norm_out, norm_recv.at[mine], norm_send_sem.at[i], norm_recv_sem.at[mine], peers[3 + i]
+        )
+
+    def norm_far_copy(i):
+        return remote(
+            norm_out, norm_recv.at[8 + col], norm_send_sem.at[7 + i], norm_recv_sem.at[8 + col], nears[i]
+        )
+
+    for i in range(7):
+        norm_copy(i).start()
+    grads_mid(0, 2)
+    grads_columns(0, 3)
+    for i in range(7):
+        norm_copy(i).wait_send()
+    for place in range(8):
+
+        @pl.when(place != mine)
+        def _():
+            pltpu.make_async_copy(norm_out, norm_recv.at[place], norm_recv_sem.at[place]).wait()
+
+    total = norm_recv[0]
+    for place in range(1, 8):
+        total = total + norm_recv[place]
+    norm_out[...] = total
+    norm_recv[8 + col] = total
+    for i in range(3):
+        norm_far_copy(i).start()
+    for m in range(3):
         grads_columns(0, m)
+    for i in range(3):
+        norm_far_copy(i).wait_send()
+    for place in range(4):
+
+        @pl.when(place != col)
+        def _():
+            pltpu.make_async_copy(norm_out, norm_recv.at[8 + place], norm_recv_sem.at[8 + place]).wait()
+
+    total = norm_recv[8]
+    for place in range(1, 4):
+        total = total + norm_recv[8 + place]
+    norm_out[...] = total
+    for m in range(4):
+        stage_sent(0, m)
     for m in range(2):
         grads_finish(1, m)
-    for m in range(4):
+    for m in (3, 0, 1, 2):
         grads_finish(0, m)
-    swap_sent(tok_buf, grad_out, 18)
-    swap_wait(tok_buf, grad_out, 18)
+    swap_sent(tok_buf, tok_out, 12)
+    swap_wait(tok_buf, tok_out, 12)
+    for i in range(2):
+        swap_sent(*grad_copy(i))
+        swap_wait(*grad_copy(i))
     swap_sent(info_in, info, 0)
     swap_sent(tok_in, tok_buf, 1)
     swap_sent(cot_in, g_all.at[own, :], 2)
@@ -1027,12 +1205,12 @@
     kv_copy(flip(par), 6).wait_send()
 
 
-def run_block(tok, cot, info, attn_half, ffn_half, norm_weight, freqs):
+def run_block(tok, cot, pos, seg, flag, attn_weight, ffn_weight, norm_weight, freqs):
     bf16, f32 = jnp.bfloat16, jnp.float32
     vmem, sem = pltpu.VMEM, pltpu.SemaphoreType.DMA
     width = tok.shape[1]
-    wide, ff_q, head_q = 2 * TOK, ffn_half.shape[2], attn_half.shape[2]
-    group = info.shape[1]
+    wide, ff_q, head_q = 2 * TOK, ffn_weight.shape[2], attn_weight.shape[2]
+    group = seg.shape[1]
     hbm = pl.BlockSpec(memory_space=pl.ANY)
     on_chip = pl.BlockSpec(memory_space=pltpu.VMEM)
     return pl.pallas_call(
@@ -1040,11 +1218,11 @@
         out_shape=(
             jax.ShapeDtypeStruct(tok.shape, bf16),
             jax.ShapeDtypeStruct(tok.shape, bf16),
-            jax.ShapeDtypeStruct((2,) + attn_half.shape, bf16),
-            jax.ShapeDtypeStruct((2,) + ffn_half.shape, bf16),
+            jax.ShapeDtypeStruct((2,) + attn_weight.shape, bf16),
+            jax.ShapeDtypeStruct((2,) + ffn_weight.shape, bf16),
             jax.ShapeDtypeStruct((8, width), f32),
         ),
-        in_specs=[hbm, hbm, hbm, hbm, hbm, on_chip, on_chip],
+        in_specs=[hbm, hbm, on_chip, on_chip, on_chip, hbm, hbm, on_chip, on_chip],
         out_specs=(hbm, hbm, hbm, hbm, on_chip),
         scratch_shapes=[
             vmem((8, group), jnp.int32),
@@ -1078,28 +1256,31 @@
             vmem((128, group), f32),
             vmem((128, group), f32),
             vmem((2, width, ff_q), bf16),
+            vmem((width, ff_q), bf16),
             vmem((4, width, head_q), bf16),
-            vmem((4, width, head_q), bf16),
-            vmem((3, 2, 256, ff_q), bf16),
-            vmem((3, 4, 256, head_q), bf16),
+            vmem((6, 2, 128, ff_q), bf16),
+            vmem((6, 4, 128, head_q), bf16),
             vmem((4, 8, width), f32),
-            vmem((5, 8, width), f32),
+            vmem((12, 8, width), f32),
             sem((4, 2)),
             sem((4, 2)),
-            sem((4, 3)),
-            sem((4, 3)),
             sem((4, 4)),
             sem((4, 4)),
-            sem((19,)),
-            sem((19,)),
+            sem((4, 4)),
+            sem((4, 4)),
+            sem((21,)),
+            sem((21,)),
             sem((6, 4)),
             sem((6, 4)),
-            sem((6, 3)),
-            sem((6, 3)),
+            sem((6, 6)),
+            sem((6, 6)),
             sem((6, 2)),
             sem((6, 2)),
-            sem((5,)),
-            sem((5,)),
+            sem((10,)),
+            sem((12,)),
+            vmem(attn_weight.shape, bf16),
+            sem((6,)),
+            vmem((8, group), jnp.int32),
         ],
         compiler_params=pltpu.CompilerParams(
             collective_id=0, has_side_effects=True, vmem_limit_bytes=VMEM_LIMIT
@@ -1108,10 +1289,75 @@
             flops=30_000_000_000, bytes_accessed=30_000_000, transcendentals=10_000_000
         ),
         name="block",
-    )(tok, cot, info, attn_half, ffn_half, norm_weight, freqs)
+    )(tok, cot, pos, seg, flag, attn_weight, ffn_weight, norm_weight, freqs)
 
 
 VMEM_LIMIT = 63 * 2**20
+
+
+def adam_kernel(grad_scale, *refs):
+    (
+        out_in,
+        dx_in,
+        attn_parts,
+        ffn_parts,
+        norm_rows,
+        attn_w,
+        attn_m,
+        attn_e,
+        ffn_w,
+        ffn_m,
+        ffn_e,
+        norm_w,
+        norm_m,
+        norm_e,
+        out_out,
+        dx_out,
+        attn_g,
+        ffn_g,
+        norm_g,
+    ) = refs[:19]
+    news = refs[19:]
+
+    def update(weight, moments, ema, grad, new_refs):
+        new_weight, new_moments, new_ema = adam_update(weight[...], moments[...], ema[...], grad * grad_scale)
+        new_refs[0][...] = new_weight
+        new_refs[1][...] = new_moments
+        new_refs[2][...] = new_ema
+
+    out_out[...] = out_in[...]
+    dx_out[...] = dx_in[...]
+    attn_g[...] = attn_parts[0].astype(jnp.float32) + attn_parts[1].astype(jnp.float32)
+    ffn_g[...] = ffn_parts[0].astype(jnp.float32) + ffn_parts[1].astype(jnp.float32)
+    norm_g[...] = norm_rows[0:4, :]
+    update(attn_w, attn_m, attn_e, attn_g[...], news[0:3])
+    update(ffn_w, ffn_m, ffn_e, ffn_g[...], news[3:6])
+    update(norm_w, norm_m, norm_e, norm_g[...], news[6:9])
+
+
+def run_adam(grad_scale, steps, out_tokens, grad_tokens, attn_parts, ffn_parts, norm_rows, *states):
+    def cut(array, dim):
+        shape = tuple(n // steps if i == dim else n for i, n in enumerate(array.shape))
+        return pl.BlockSpec(shape, lambda i: tuple(i if n == dim else 0 for n in range(len(shape))))
+
+    def same(array):
+        return pl.BlockSpec(array.shape, lambda i: (0,) * array.ndim)
+
+    attn, ffn, norm = states[0:3], states[3:6], states[6:9]
+    state_specs = [cut(a, a.ndim - 2) for a in attn + ffn] + [same(a) for a in norm]
+    in_specs = [cut(out_tokens, 0), cut(grad_tokens, 0), cut(attn_parts, 2), cut(ffn_parts, 2), same(norm_rows)]
+    heads = [out_tokens, grad_tokens, attn[0], ffn[0], norm[0]]
+    head_specs = [cut(out_tokens, 0), cut(grad_tokens, 0), cut(attn[0], 1), cut(ffn[0], 1), same(norm[0])]
+    return pl.pallas_call(
+        lambda *refs: adam_kernel(grad_scale, *refs),
+        grid=(steps,),
+        out_shape=tuple(jax.ShapeDtypeStruct(a.shape, a.dtype) for a in heads + list(states)),
+        in_specs=in_specs + state_specs,
+        out_specs=tuple(head_specs + state_specs),
+        compiler_params=pltpu.CompilerParams(vmem_limit_bytes=VMEM_LIMIT),
+        cost_estimate=pl.CostEstimate(flops=8_000_000, bytes_accessed=16_000_000, transcendentals=800_000),
+        name="adam",
+    )(out_tokens, grad_tokens, attn_parts, ffn_parts, norm_rows, *states)
 
 
 def local_fast(
@@ -1134,47 +1380,35 @@
     group = segment_ids.shape[1]
     exponent = -2.0 * (np.arange(width) // 2) / width
     freqs = jnp.asarray(np.tile((10000.0**exponent).astype(np.float32), (8, 1)))
-    info = jnp.zeros((8, group), jnp.int32)
-    info = info.at[0].set(segment_ids[0])
-    info = info.at[1, : positions.shape[1]].set(positions[0])
-    info = info.at[2, : spatial_flag.shape[1]].set(spatial_flag[0])
     grad_scale = float(group * lax.axis_size("dp")) ** (-0.5)
     out_tokens, grad_tokens, attn_parts, ffn_parts, norm_rows = run_block(
         tokens,
         cotangent,
-        info,
-        attn_weight.astype(jnp.bfloat16),
-        ffn_weight.astype(jnp.bfloat16),
+        positions,
+        segment_ids,
+        spatial_flag,
+        attn_weight,
+        ffn_weight,
         norm_weight,
         freqs,
     )
-    attn_grad = attn_parts[0].astype(jnp.float32) + attn_parts[1].astype(jnp.float32)
-    ffn_grad = ffn_parts[0].astype(jnp.float32) + ffn_parts[1].astype(jnp.float32)
-    norm_grad = norm_rows[:4]
-    attn_new, attn_mom_new, attn_ema_new = adam_update(
-        attn_weight, attn_moments, attn_ema, attn_grad * grad_scale
-    )
-    ffn_new, ffn_mom_new, ffn_ema_new = adam_update(
-        ffn_weight, ffn_moments, ffn_ema, ffn_grad * grad_scale
-    )
-    norm_new, norm_mom_new, norm_ema_new = adam_update(
-        norm_weight, norm_moments, norm_ema, norm_grad * grad_scale
-    )
-    return (
+    return run_adam(
+        grad_scale,
+        4,
         out_tokens,
         grad_tokens,
-        attn_grad,
-        ffn_grad,
-        norm_grad,
-        attn_new,
-        attn_mom_new,
-        attn_ema_new,
-        ffn_new,
-        ffn_mom_new,
-        ffn_ema_new,
-        norm_new,
-        norm_mom_new,
-        norm_ema_new,
+        attn_parts,
+        ffn_parts,
+        norm_rows,
+        attn_weight,
+        attn_moments,
+        attn_ema,
+        ffn_weight,
+        ffn_moments,
+        ffn_ema,
+        norm_weight,
+        norm_moments,
+        norm_ema,
     )
 
 

time: 263 us -> 208 us (0.79)
  Pallas kernels: 240 us -> 207 us
  other arithmetic: 15.2 us -> 0 us
  local copies, waits for them, and re-layouts: 4.67 us -> 0 us
    pallas_call x1, Pallas kernels: 240 us -> 198 us  [run_block(): pl.pallas_call(block_kernel, out_shape=(jax.ShapeDtypeStruct(tok.shape, b...]
    pallas_call x0 -> x1, Pallas kernels: none -> 8.57 us  [run_adam(): pl.pallas_call(lambda *refs: adam_kernel(grad_scale, *refs), grid=(steps,...]
    add x5 -> x0, other arithmetic: 8.12 us -> none  [the longest x3 5.68 us: adam_update(): new_ema = ema_value * ema_weight + (1.0 - ema_value) * new_weight]
    unnamed x38 -> x0, local copies, waits for them, and re-layouts: 4.17 us -> none
    convert_element_type x2 -> x0, other arithmetic: 3.88 us -> none  [the longest x1 2.11 us: local_fast(): ffn_weight.astype(jnp.bfloat16)]
    another operation x4 -> x0, other arithmetic: 3.18 us -> none  [adam_update(): return (new_weight, jnp.stack([first_mom, second_mom]), new_ema)]
where the time goes in v2:
time: 208 us; the launch traced here: 207 us
  Pallas kernels  207 us (100%)
    pallas_call x1, Pallas kernels, run_block(): pl.pallas_call(block_kernel, out_shape=(jax.ShapeDtypeStruct(tok.shape, b...  198 us
    pallas_call x1, Pallas kernels, run_adam(): pl.pallas_call(lambda *refs: adam_kernel(grad_scale, *refs), grid=(steps,...  8.57 us

profile of v2, /device:TPU:5, one launch (start us, length us, event | category | flops | bytes accessed | tf_op | source)
XLA Modules:
  0.0 207.5 jit_solution(2470660706640399579)
XLA Ops:
  0.6 198.1 %block.1 = (bf16[256,1024]{1,0:T(8,128)(2,1)}, bf16[256,1024]{1,0:T(8,128)(2,1)}, bf16[2,4,128,256]{3,2,1,0:T(8,128)(2,1)}, bf16[2,2,128,1024]{3,2,1,0:T(8,128)(2,1)}, f32[8,1024]{1,0:T(8,128)}) custom-call(bf16[256,1024]{1,0:T(8,128)(2,1)} %tok_in.1, bf16[256,1024]{1,0:T(8,128)(2,1)} %cot_in.1, s32[1,256]{1,0:T(1,128)} %pos_in.1, s32[1,1024]{1,0:T(1,128)} %seg_in.1, ...), custom_call_target="tpu_custom_call" | custom-call | flops 30000001024 | bytes 30000000 | tf_op jit(solution)/shard_map/block/pallas_call | solution.py:1216
  198.7 8.6 %adam.1 = (bf16[256,1024]{1,0:T(8,128)(2,1)}, bf16[256,1024]{1,0:T(8,128)(2,1)}, f32[4,128,256]{2,1,0:T(8,128)}, f32[2,128,1024]{2,1,0:T(8,128)}, f32[4,1024]{1,...) custom-call(bf16[256,1024]{1,0:T(8,128)(2,1)} %get-tuple-element.19., ...), custom_call_target="tpu_custom_call" | custom-call | flops 8000000 | bytes 16000000 | tf_op jit(solution)/shard_map/adam/pallas_call | solution.py:1351

commit v3 on v2

--- a/solution.py
+++ b/solution.py
@@ -292,6 +292,15 @@
     cosine = (cosine + 4.166664568298827e-2) * square * square - 0.5 * square + 1.0
     value = jnp.where((quadrant & 1) == 1, cosine, sine)
     return jnp.where((quadrant & 2) == 2, -value, value)
+
+
+def gelu_gate(hidden, bell):
+    step = 1.0 / (1.0 + np.float32(0.3275911 * np.sqrt(0.5)) * jnp.abs(hidden))
+    tail = np.float32(0.5 * 1.061405429) * step - np.float32(0.5 * 1.453152027)
+    tail = tail * step + np.float32(0.5 * 1.421413741)
+    tail = tail * step - np.float32(0.5 * 0.284496736)
+    tail = (tail * step + np.float32(0.5 * 0.254829592)) * step * bell
+    return jnp.where(hidden < 0.0, tail, 1.0 - tail)
 
 
 def normalized(rows):
@@ -505,13 +514,10 @@
                 one_copy(piece, k).wait_send()
 
     def two_copy(piece, k):
-        if k < 2:
-            rows, target = aligned(col * 256, 256), nears[k]
-        elif k == 2:
-            rows, target = aligned(near_cols[0] * 256, 128), nears[1]
-        else:
-            rows, target = aligned(near_cols[1] * 256 + 128, 128), nears[0]
+        which = (col, col, col, col, near_cols[0], near_cols[1])[k]
+        rows = aligned(which * 256 + (0, 1, 1, 0, 0, 1)[k] * 128, 128)
         view = piece_view(piece, core, rows)
+        target = nears[(0, 1, 0, 1, 1, 0)[k]]
         return remote(view, view, two_send.at[piece, k], two_recv.at[piece, k], target)
 
     def sib_copy(piece, k):
@@ -525,18 +531,20 @@
             pltpu.make_async_copy(
                 piece_source(piece), piece_view(piece, core, rows), one_recv.at[piece, c0]
             ).wait()
-        for k in range(2):
+        for k in range(4):
             two_copy(piece, k).start()
         sib_copy(piece, 0).start()
 
     def relay(piece):
         for k in range(2):
             two_copy(piece, k).wait_recv()
-            two_copy(piece, k + 2).start()
+            two_copy(piece, k + 4).start()
+
+    def relay_last(piece):
+        for k in range(2):
+            two_copy(piece, k + 2).wait_recv()
             sib_copy(piece, k + 1).start()
-
-    def relay_last(piece):
-        for k in range(2, 4):
+        for k in range(4, 6):
             two_copy(piece, k).wait_recv()
         sib_copy(piece, 3).start()
 
@@ -545,8 +553,9 @@
             sib_copy(piece, k).wait_recv()
 
     def sent(piece):
+        for k in range(6):
+            two_copy(piece, k).wait_send()
         for k in range(4):
-            two_copy(piece, k).wait_send()
             sib_copy(piece, k).wait_send()
 
     swap_in(info_in, info, 0)
@@ -614,8 +623,8 @@
 
     spread(0)
     relay(0)
+    spread(1)
     relay_last(0)
-    spread(1)
     pl.when(jnp.logical_not(home))(embed_cells)
     one_start(2)
     ready(0)
@@ -645,9 +654,9 @@
     project(flip(par))
     kv_copy(flip(par), 6).start()
     relay_last(1)
+    spread(2)
     kv_copy(par, 5).wait_recv()
     kv_copy(flip(par), 6).wait_recv()
-    spread(2)
 
     lane_half = lax.broadcasted_iota(jnp.int32, (TOK, 128), 1)
     lane_masks = (lane_half < HD, lane_half >= HD)
@@ -696,9 +705,22 @@
 
         lax.fori_loop(0, width // WIDE, step, 0)
 
-    def product_send(product, scale, send_buf, recv_buf, index):
-        product_fill(product, scale, send_buf)
-        remote(send_buf, recv_buf, act_send.at[index], act_recv.at[index], pair).start()
+    def half_copy(i, index):
+        rows = pl.ds(i * 128, 128)
+        return remote(
+            send_a.at[rows, :], recv_a.at[rows, :], act_send.at[index + i], act_recv.at[index + i], pair
+        )
+
+    def product_halves(product, scale, index):
+        for i in range(2):
+            part = product(aligned(flip(par) * TOK + i * 128, 128), None) * scale
+            send_a[i * 128 : (i + 1) * 128, :] = part.astype(jnp.bfloat16)
+            half_copy(i, index).start()
+
+    def pair_half(buf, i, index):
+        rows = aligned(par * TOK + i * 128, 128)
+        view = buf.at[rows, :]
+        return remote(view, view, act_send.at[index + i], act_recv.at[index + i], pair)
 
     def product_keep(product, scale, acc):
         def step(n, carry):
@@ -712,17 +734,16 @@
         remote(send_buf, recv_buf, act_send.at[index], act_recv.at[index], pair).wait()
 
     def out_product(rows, n):
-        outs = aligned(n * WIDE, WIDE)
+        outs = slice(None) if n is None else aligned(n * WIDE, WIDE)
         total = contract(att[0, rows, :], attn_w[0, 3, outs, :], 1, 1)
         return total + contract(att[1, rows, :], attn_w[1, 3, outs, :], 1, 1)
 
-    product_send(out_product, out_scale, send_a, recv_a, 7)
+    product_halves(out_product, out_scale, 21)
     relay(2)
     attend_rows(par)
     relay_last(2)
     spread(3)
     product_keep(out_product, out_scale, acc_a)
-    split_wait(send_a, recv_a, 7)
 
     def norm_second(step, carry):
         rows = aligned(step * CHUNK, CHUNK)
@@ -733,8 +754,10 @@
         h_two[row, :] = (unit * norm_in[2:3, :] + norm_in[3:4, :]).astype(jnp.bfloat16)
         return carry
 
-    lax.fori_loop(0, TOK // CHUNK, norm_second, 0)
-    pair_copy(h_two, 8).start()
+    for i in range(2):
+        half_copy(i, 21).wait()
+        lax.fori_loop(4 * i, 4 * i + 4, norm_second, 0)
+        pair_half(h_two, i, 23).start()
 
     @pl.when(jnp.logical_not(home))
     def _():
@@ -750,10 +773,11 @@
             h = lax.div(i, 2)
             lanes = aligned(lax.rem(i, 2) * 512, 512)
             hidden = contract(h_two[rows, :], ffn_w[h, 0, :, lanes], 1, 0) * scale_d
-            gate = 0.5 + 0.5 * lax.erf(hidden * np.float32(np.sqrt(0.5)))
+            bell = jnp.exp(-0.5 * hidden * hidden)
+            gate = gelu_gate(hidden, bell)
             act[h, rows, lanes] = (hidden * gate).astype(jnp.bfloat16)
-            bell = jnp.exp(-0.5 * hidden * hidden) * np.float32(1.0 / np.sqrt(2.0 * np.pi))
-            d_hid[h, rows, lanes] = (gate + hidden * bell).astype(jnp.bfloat16)
+            slope = gate + hidden * bell * np.float32(1.0 / np.sqrt(2.0 * np.pi))
+            d_hid[h, rows, lanes] = slope.astype(jnp.bfloat16)
             return carry
 
         lax.fori_loop(0, 4, step, 0)
@@ -772,7 +796,7 @@
         lax.fori_loop(0, 4, step, 0)
 
     def hid_product(rows, n):
-        outs = aligned(n * WIDE, WIDE)
+        outs = slice(None) if n is None else aligned(n * WIDE, WIDE)
         total = contract(d_hid[0, rows, :], ffn_w[0, 0, outs, :], 1, 1)
         return total + contract(d_hid[1, rows, :], ffn_w[1, 0, outs, :], 1, 1)
 
@@ -781,185 +805,176 @@
         total = contract(act[0, rows, :], ffn_w[0, 1, outs, :], 1, 1)
         return total + contract(act[1, rows, :], ffn_w[1, 1, outs, :], 1, 1)
 
-    def grad_tile(kind, m, h, tile):
-        cells = aligned(tile * 256, 256)
-        if kind == 0:
-            left = h_one[:, cells] if m < 3 else d_mid_all[:, cells]
-            right = d_qkv[m, h] if m < 3 else att[h]
-            return contract(left, right, 0, 0) * (scale_d if m < 3 else out_scale)
-        left = h_two[:, cells] if m == 0 else g_all[:, cells]
-        right = d_hid[h] if m == 0 else act[h]
-        return contract(left, right, 0, 0) * (scale_d if m == 0 else scale_f)
-
-    def stage_view(kind, m, rows):
-        return stage.at[rows, pl.ds(m * 256, 256)] if kind == 0 else stage.at[rows, :]
-
-    def sum_view(kind, m, rows):
-        return attn_sum.at[m, rows, :] if kind == 0 else ffn_sum.at[m, rows, :]
-
-    def slot(kind, m):
-        return m if kind == 0 else 4 + m
-
-    def tile_copy(kind, m, tile):
-        rows = aligned(tile * 256, 256)
-        index = slot(kind, m)
+    def grad_product(matrix, h, n):
+        if matrix < 3:
+            return contract(h_one[...], d_qkv[matrix, h], 0, 0) * scale_d
+        if matrix == 3:
+            return contract(d_mid_all[...], att[h], 0, 0) * out_scale
+        lanes = aligned(n * 256, 256)
+        if matrix == 4:
+            return contract(h_two[...], d_hid[h, :, lanes], 0, 0) * scale_d
+        return contract(g_all[...], act[h, :, lanes], 0, 0) * scale_f
+
+    def tiles(matrix):
+        return 1 if matrix < 4 else 4
+
+    def stage_view(matrix, n):
+        return stage.at[:, aligned((matrix if matrix < 4 else n) * 256, 256)]
+
+    def tile_view(matrix, n):
+        return attn_sum.at[matrix] if matrix < 4 else ffn_sum.at[matrix - 4, :, aligned(n * 256, 256)]
+
+    def tile_copy(matrix, n):
         return remote(
-            stage_view(kind, m, rows),
-            sum_view(kind, m, rows),
-            grad_sib_send.at[index, tile],
-            grad_sib_recv.at[index, tile],
+            stage_view(matrix, n),
+            tile_view(matrix, n),
+            grad_sib_send.at[matrix, n],
+            grad_sib_recv.at[matrix, n],
             sib,
         )
 
-    def grads_sibling(kind, m):
-        def step(tile, carry):
-            rows = aligned(tile * 256, 256)
-            view = stage_view(kind, m, rows)
-            view[...] = grad_tile(kind, m, flip(core), tile).astype(jnp.bfloat16)
-            tile_copy(kind, m, tile).start()
+    def grads_sibling(matrix):
+        def step(n, carry):
+            view = stage_view(matrix, n)
+            view[...] = grad_product(matrix, flip(core), n).astype(jnp.bfloat16)
+            tile_copy(matrix, n).start()
             return carry
 
-        lax.fori_loop(0, 4, step, 0)
-
-    def tile_place(k):
-        to_x = 1 - lax.div(k, 2)
-        to_y = 1 - lax.rem(k, 2)
-        x_new = x_bit + to_x - 2 * x_bit * to_x
-        y_new = y_bit + to_y - 2 * y_bit * to_y
-        return 2 * y_new + x_new
+        if tiles(matrix) == 1:
+            step(0, 0)
+        else:
+            lax.fori_loop(0, tiles(matrix), step, 0)
+
+    def stage_sent(matrix):
+        for n in range(tiles(matrix)):
+            tile_copy(matrix, n).wait_send()
+
+    def grads_own(matrix):
+        def step(n, carry):
+            total = grad_product(matrix, core, n)
+            tile_copy(matrix, n).wait_recv()
+            view = tile_view(matrix, n)
+            view[...] = (total + view[...].astype(jnp.float32)).astype(jnp.bfloat16)
+            return carry
+
+        if tiles(matrix) == 1:
+            step(0, 0)
+        else:
+            lax.fori_loop(0, tiles(matrix), step, 0)
+
+    def sum_view(group, rows):
+        if group == 0:
+            return attn_sum.at[0:3, rows, :]
+        return attn_sum.at[3, rows, :] if group == 1 else ffn_sum.at[group - 2, rows, :]
 
     def box_rows(k):
         place = (near_cols[2], near_cols[2], near_cols[0], near_cols[1], near_cols[0], near_cols[1])[k]
         return aligned(place * 256 + (0, 1, 0, 1, 1, 0)[k] * 128, 128)
 
-    def box_view(kind, m, k):
-        return attn_box.at[k, m] if kind == 0 else ffn_box.at[k, m]
-
-    def box_copy(kind, m, k):
-        index = slot(kind, m)
+    def box_view(group, k):
+        if group == 0:
+            return attn_box.at[k, 0:3]
+        return attn_box.at[k, 3] if group == 1 else ffn_box.at[k, group - 2]
+
+    def box_copy(group, k):
         return remote(
-            sum_view(kind, m, box_rows(k)),
-            box_view(kind, m, k),
-            grad_box_send.at[index, k],
-            grad_box_recv.at[index, k],
+            sum_view(group, box_rows(k)),
+            box_view(group, k),
+            grad_box_send.at[group, k],
+            grad_box_recv.at[group, k],
             nears[k % 2],
         )
 
-    def stage_sent(kind, m):
-        for tile in range(4):
-            tile_copy(kind, m, tile).wait_send()
-
-    def grads_own(kind, m):
-        def tile(k):
-            place = tile_place(k)
-            total = grad_tile(kind, m, core, place)
-            tile_copy(kind, m, place).wait_recv()
-            view = sum_view(kind, m, aligned(place * 256, 256))
-            view[...] = (total + view[...].astype(jnp.float32)).astype(jnp.bfloat16)
-
-        def step(k, carry):
-            tile(k)
-
-            @pl.when(k == 0)
-            def _():
-                box_copy(kind, m, 0).start()
-                box_copy(kind, m, 1).start()
-
-            @pl.when(k == 1)
-            def _():
-                box_copy(kind, m, 2).start()
-
-            @pl.when(k == 2)
-            def _():
-                box_copy(kind, m, 3).start()
-
-            return carry
-
-        lax.fori_loop(0, 4, step, 0)
-
-    def grads_mid(kind, m):
+    def grads_start(group):
+        for k in range(4):
+            box_copy(group, k).start()
+
+    def grads_mid(group):
         for k, came in ((4, 1), (5, 0)):
-            box_copy(kind, m, came).wait_recv()
-            view = sum_view(kind, m, box_rows(k))
-            box = box_view(kind, m, came)
+            box_copy(group, came).wait_recv()
+            view = sum_view(group, box_rows(k))
+            box = box_view(group, came)
             view[...] = (view[...].astype(jnp.float32) + box[...].astype(jnp.float32)).astype(jnp.bfloat16)
-            box_copy(kind, m, k).start()
-
-    def own_copy(kind, m, c0):
-        rows = aligned(col * 256 + c0 * 128, 128)
-        dst = attn_parts.at[half, m] if kind == 0 else ffn_parts.at[half, m]
-        index = slot(kind, m)
+            box_copy(group, k).start()
+
+    def part_view(group, k):
+        if group == 0:
+            return attn_parts.at[k, 0:3]
+        return attn_parts.at[k, 3] if group == 1 else ffn_parts.at[k, group - 2]
+
+    def own_rows(c0):
+        return aligned(col * 256 + c0 * 128, 128)
+
+    def own_copy(group, c0):
         return remote(
-            sum_view(kind, m, rows),
-            dst,
-            grad_own_send.at[index, c0],
-            grad_own_recv.at[index, half],
+            sum_view(group, own_rows(c0)),
+            part_view(group, half),
+            grad_own_send.at[group, c0],
+            grad_own_recv.at[group, half],
             (d - core + c0, quarter),
         )
 
     def own_is_here(c0):
         return jnp.logical_and(core == c0, t == quarter)
 
-    def grads_columns(kind, m):
+    def grads_columns(group):
         for c0, came in ((0, (2, 5)), (1, (3, 4))):
             for k in came:
-                box_copy(kind, m, k).wait_recv()
-            view = sum_view(kind, m, aligned(col * 256 + c0 * 128, 128))
+                box_copy(group, k).wait_recv()
+            view = sum_view(group, own_rows(c0))
             total = view[...].astype(jnp.float32)
             for k in came:
-                total = total + box_view(kind, m, k)[...].astype(jnp.float32)
+                total = total + box_view(group, k)[...].astype(jnp.float32)
             view[...] = total.astype(jnp.bfloat16)
-        for c0 in range(2):
 
             @pl.when(own_is_here(c0))
             def _():
-                rows = aligned(col * 256 + c0 * 128, 128)
-                dst = attn_parts.at[half, m] if kind == 0 else ffn_parts.at[half, m]
                 pltpu.make_async_copy(
-                    sum_view(kind, m, rows), dst, grad_own_recv.at[slot(kind, m), half]
+                    sum_view(group, own_rows(c0)), part_view(group, half), grad_own_recv.at[group, half]
                 ).start()
 
             @pl.when(jnp.logical_not(own_is_here(c0)))
             def _():
-                own_copy(kind, m, c0).start()
-
-    def grads_finish(kind, m):
-        index = slot(kind, m)
+                own_copy(group, c0).start()
+
+    def grads_finish(group):
         for k in range(2):
-            src = sum_view(kind, m, aligned(col * 256, 128))
-            dst = attn_parts.at[k, m] if kind == 0 else ffn_parts.at[k, m]
-            pltpu.make_async_copy(src, dst, grad_own_recv.at[index, k]).wait()
+            pltpu.make_async_copy(
+                sum_view(group, own_rows(0)), part_view(group, k), grad_own_recv.at[group, k]
+            ).wait()
         for k in range(6):
-            box_copy(kind, m, k).wait_send()
+            box_copy(group, k).wait_send()
         for c0 in range(2):
 
             @pl.when(jnp.logical_not(own_is_here(c0)))
             def _():
-                own_copy(kind, m, c0).wait_send()
+                own_copy(group, c0).wait_send()
 
     feed_up(par)
     relay(3)
-    pair_copy(h_two, 8).wait_recv()
+    for i in range(2):
+        pair_half(h_two, i, 23).wait_recv()
     feed_up(flip(par))
     relay_last(3)
     pair_copy(g_all, 4).wait_recv()
-    grads_sibling(1, 1)
+    grads_sibling(5)
+    grads_own(5)
+    grads_start(3)
     ready(3)
     feed_back(flip(par))
-    product_send(hid_product, scale_d, send_a, recv_a, 9)
+    product_halves(hid_product, scale_d, 25)
     feed_back(par)
-    grads_own(1, 1)
-    stage_sent(1, 1)
-    grads_sibling(1, 0)
+    stage_sent(5)
+    grads_sibling(4)
+    grads_mid(3)
+    grads_own(4)
+    grads_start(2)
     product_keep(hid_product, scale_d, acc_a)
-    grads_mid(1, 1)
-    grads_own(1, 0)
     for piece in range(4):
         one_sent(piece)
         sent(piece)
     product_fill(down_product, scale_f, send_b)
 
-    split_wait(send_a, recv_a, 9)
 
     def back_norm(step, base, gain, add, acc, out):
         rows = aligned(step * CHUNK, CHUNK)
@@ -985,8 +1000,10 @@
         return carry
 
     norm_acc[...] = jnp.zeros_like(norm_acc)
-    lax.fori_loop(0, TOK // CHUNK, back_second, 0)
-    pair_copy(d_mid_all, 11).start()
+    for i in range(2):
+        half_copy(i, 25).wait()
+        lax.fori_loop(4 * i, 4 * i + 4, back_second, 0)
+        pair_half(d_mid_all, i, 27).start()
     product_keep(down_product, scale_f, acc_b)
 
     def back_out(first):
@@ -1052,16 +1069,16 @@
         return remote(kv_send.at[jj], kv_recv.at[jj], act_send.at[13 + jj], act_recv.at[13 + jj], sib)
 
     back_out(par)
-    grads_columns(1, 1)
-    grads_mid(1, 0)
     attend_back_rows(par, False)
-    pair_copy(d_mid_all, 11).wait_recv()
+    grads_columns(3)
+    grads_mid(2)
+    for i in range(2):
+        pair_half(d_mid_all, i, 27).wait_recv()
     remote(send_b, recv_b, act_send.at[10], act_recv.at[10], pair).start()
     back_out(flip(par))
     attend_back_rows(flip(par), True)
-    grads_columns(1, 0)
-    stage_sent(1, 0)
-    grads_sibling(0, 3)
+    stage_sent(4)
+    grads_sibling(3)
 
     def join_kv(jj, carry):
         kv_grad_copy(jj).wait()
@@ -1083,23 +1100,19 @@
                 total = part if total is None else total + part
         return total
 
-    def first_copy(i):
-        rows = pl.ds(i * 128, 128)
-        return remote(
-            send_a.at[rows, :], recv_a.at[rows, :], act_send.at[19 + i], act_recv.at[19 + i], pair
-        )
-
-    for i in range(2):
-        part = first_product(aligned(flip(par) * TOK + i * 128, 128), None) * scale_d
-        send_a[i * 128 : (i + 1) * 128, :] = part.astype(jnp.bfloat16)
-        first_copy(i).start()
-
-    for m in range(3):
-        grads_sibling(0, m)
+    product_halves(first_product, scale_d, 19)
+    grads_columns(2)
+
+    for matrix in range(3):
+        grads_sibling(matrix)
     product_keep(first_product, scale_d, acc_a)
-    grads_own(0, 3)
-    for m in range(3):
-        grads_own(0, m)
+
+    grads_own(3)
+    grads_start(1)
+    for matrix in range(3):
+        grads_own(matrix)
+    grads_mid(1)
+    grads_start(0)
 
     split_wait(send_b, recv_b, 10)
 
@@ -1111,10 +1124,9 @@
 
     lax.fori_loop(0, TOK // CHUNK, finish_out, 0)
     swap_in(tok_buf, tok_out, 12)
-
-
-    for m in (3, 0, 1):
-        grads_mid(0, m)
+    grads_mid(0)
+    grads_columns(1)
+
     def back_first(step, carry):
         def out(rows, result):
             send_b[rows, :] = result.astype(jnp.bfloat16)
@@ -1130,9 +1142,8 @@
         return send_b.at[rows, :], grad_out.at[rows, :], 17 + i
 
     for i in range(2):
-        first_copy(i).wait()
+        half_copy(i, 19).wait()
         lax.fori_loop(4 * i, 4 * i + 4, back_first, 0)
-        swap_in(*grad_copy(i))
 
     for row in range(4):
         norm_out[row : row + 1, :] = jnp.sum(norm_acc[row], axis=0, keepdims=True)
@@ -1152,8 +1163,9 @@
 
     for i in range(7):
         norm_copy(i).start()
-    grads_mid(0, 2)
-    grads_columns(0, 3)
+    for i in range(2):
+        swap_in(*grad_copy(i))
+    grads_columns(0)
     for i in range(7):
         norm_copy(i).wait_send()
     for place in range(8):
@@ -1169,8 +1181,6 @@
     norm_recv[8 + col] = total
     for i in range(3):
         norm_far_copy(i).start()
-    for m in range(3):
-        grads_columns(0, m)
     for i in range(3):
         norm_far_copy(i).wait_send()
     for place in range(4):
@@ -1183,12 +1193,10 @@
     for place in range(1, 4):
         total = total + norm_recv[8 + place]
     norm_out[...] = total
-    for m in range(4):
-        stage_sent(0, m)
-    for m in range(2):
-        grads_finish(1, m)
-    for m in (3, 0, 1, 2):
-        grads_finish(0, m)
+    for matrix in range(4):
+        stage_sent(matrix)
+    for group in (3, 2, 1, 0):
+        grads_finish(group)
     swap_sent(tok_buf, tok_out, 12)
     swap_wait(tok_buf, tok_out, 12)
     for i in range(2):
@@ -1199,8 +1207,9 @@
     swap_sent(cot_in, g_all.at[own, :], 2)
     pair_copy(h_one, 3).wait_send()
     pair_copy(g_all, 4).wait_send()
-    pair_copy(h_two, 8).wait_send()
-    pair_copy(d_mid_all, 11).wait_send()
+    for i in range(2):
+        pair_half(h_two, i, 23).wait_send()
+        pair_half(d_mid_all, i, 27).wait_send()
     kv_copy(par, 5).wait_send()
     kv_copy(flip(par), 6).wait_send()
 
@@ -1264,18 +1273,18 @@
             vmem((12, 8, width), f32),
             sem((4, 2)),
             sem((4, 2)),
+            sem((4, 6)),
+            sem((4, 6)),
             sem((4, 4)),
             sem((4, 4)),
-            sem((4, 4)),
-            sem((4, 4)),
-            sem((21,)),
-            sem((21,)),
+            sem((29,)),
+            sem((29,)),
             sem((6, 4)),
             sem((6, 4)),
-            sem((6, 6)),
-            sem((6, 6)),
-            sem((6, 2)),
-            sem((6, 2)),
+            sem((4, 6)),
+            sem((4, 6)),
+            sem((4, 2)),
+            sem((4, 2)),
             sem((10,)),
             sem((12,)),
             vmem(attn_weight.shape, bf16),
@@ -1394,7 +1403,7 @@
     )
     return run_adam(
         grad_scale,
-        4,
+        2,
         out_tokens,
         grad_tokens,
         attn_parts,

time: 208 us -> 199 us (0.957)
  Pallas kernels: 207 us -> 196 us
    pallas_call x1, Pallas kernels: 198 us -> 189 us  [run_block(): pl.pallas_call(block_kernel, out_shape=(jax.ShapeDtypeStruct(tok.shape, b...]
where the time goes in v3:
time: 199 us; the launch traced here: 197 us
  Pallas kernels  196 us (98%)
    pallas_call x1, Pallas kernels, run_block(): pl.pallas_call(block_kernel, out_shape=(jax.ShapeDtypeStruct(tok.shape, b...  189 us
    pallas_call x1, Pallas kernels, run_adam(): pl.pallas_call(lambda *refs: adam_kernel(grad_scale, *refs), grid=(steps,...  7.72 us

profile of v3, /device:TPU:5, one launch (start us, length us, event | category | flops | bytes accessed | tf_op | source)
XLA Modules:
  0.0 197.2 jit_solution(15123261583577706567)
XLA Ops:
  0.6 188.7 %block.1 = (bf16[256,1024]{1,0:T(8,128)(2,1)}, bf16[256,1024]{1,0:T(8,128)(2,1)}, bf16[2,4,128,256]{3,2,1,0:T(8,128)(2,1)}, bf16[2,2,128,1024]{3,2,1,0:T(8,128)(2,1)}, f32[8,1024]{1,0:T(8,128)}) custom-call(bf16[256,1024]{1,0:T(8,128)(2,1)} %tok_in.1, bf16[256,1024]{1,0:T(8,128)(2,1)} %cot_in.1, s32[1,256]{1,0:T(1,128)} %pos_in.1, s32[1,1024]{1,0:T(1,128)} %seg_in.1, ...), custom_call_target="tpu_custom_call" | custom-call | flops 30000001024 | bytes 30000000 | tf_op jit(solution)/shard_map/block/pallas_call | solution.py:1225
  189.3 7.7 %adam.1 = (bf16[256,1024]{1,0:T(8,128)(2,1)}, bf16[256,1024]{1,0:T(8,128)(2,1)}, f32[4,128,256]{2,1,0:T(8,128)}, f32[2,128,1024]{2,1,0:T(8,128)}, f32[4,1024]{1,...) custom-call(bf16[256,1024]{1,0:T(8,128)(2,1)} %get-tuple-element.19., ...), custom_call_target="tpu_custom_call" | custom-call | flops 8000000 | bytes 16000000 | tf_op jit(solution)/shard_map/adam/pallas_call | solution.py:1360
